TPU v7x, 512 devices: a whole 4x4x16 slice. The times are simulated.
512 devices in a mesh: group: 64 (over z, x), tensor: 8 (over y, core).
Axes of the slice: x: 4, y: 4, z: 16, core: 2. Of those that a mesh axis runs over, the one named last changes fastest.
Arguments:
- tokens: bfloat16 [32768, 2048], P('group', 'tensor')
- w_query: bfloat16 [2048, 2048], P('group', 'tensor'), may hold values from -0.125 to 0.125
- w_key: bfloat16 [2048, 2048], P('group', 'tensor'), may hold values from -0.125 to 0.125
- w_value: bfloat16 [2048, 2048], P('group', 'tensor'), may hold values from -0.125 to 0.125
- w_out: bfloat16 [2048, 2048], P('tensor', 'group'), may hold values from -0.125 to 0.125
- prefix_cache: bfloat16 [64, 2, 512, 2048], P('group', None, None, 'tensor')
- prefix_len: int32 [64], P('group'), may hold values from 0 to 512, as said below
- owners: int32 [4096, 1], P('group'), may hold values from 0 to 63; in each aligned block of 64 rows (0 to 63, 64 to 127, ...) at most 2 rows name the same one
Outputs:
- attn_out: bfloat16 [32768, 2048], P('group', 'tensor')
- decode_cache: bfloat16 [64, 128, 2, 16, 2048], P('group', None, None, None, 'tensor')
Inputs may be any that keep to these rules, and one draw needn't show every extreme that they name: `owners`: every prompt sends at most 2 blocks to one owner, and exactly 2 to some owner. `prefix_len`: some prompt fills all 512 slots.
All inputs are finite; a program needn't handle non-finite values.
Results may differ from a plain program's by a relative error of at most 0.02.
The roundings to bfloat16 on the way count: a program that leaves them out, or rounds other values in their place, can miss the bound.
Values may be sent and summed in bfloat16 or wider, within the bound.
A program may use at most 64 MiB of HBM per device.

v0:
```python
import jax
import jax.numpy as jnp
from jax import lax
from jax.sharding import PartitionSpec as P

HD = 128


def attend(query, new_key, new_value, prefix, plen):
    rows, width = query.shape
    heads = width // HD
    pre = prefix.shape[1]
    keys = jnp.concatenate([prefix[0], new_key], 0).reshape(pre + rows, heads, HD)
    values = jnp.concatenate([prefix[1], new_value], 0).reshape(pre + rows, heads, HD)
    qmat = query.reshape(rows, heads, HD)
    scores = jnp.einsum("chd,khd->hck", qmat, keys, preferred_element_type=jnp.float32) * HD ** (
        -0.5
    )
    kpos = jnp.arange(pre + rows)[None, :]
    cpos = jnp.arange(rows)[:, None]
    valid = jnp.where(kpos < pre, kpos < plen, kpos - pre <= cpos)
    scores = jnp.where(valid[None], scores, -jnp.inf)
    top = jnp.max(scores, axis=-1, keepdims=True)
    expo = jnp.exp(scores - top)
    weights = (expo / jnp.sum(expo, axis=-1, keepdims=True)).astype(jnp.bfloat16)
    context = jnp.einsum("hck,khd->chd", weights, values, preferred_element_type=jnp.float32)
    return context.astype(jnp.bfloat16).reshape(rows, width)


def body(tokens, w_query, w_key, w_value, w_out, prefix_cache, prefix_len, owners):
    whole = lax.all_gather(tokens, "tensor", axis=1, tiled=True)
    rows = whole.shape[0]
    local_width = w_query.shape[1]
    pieces = (
        lax.all_gather(w_query, "group", axis=0, tiled=True),
        lax.all_gather(w_key, "group", axis=0, tiled=True),
        lax.all_gather(w_value, "group", axis=0, tiled=True),
    )
    query, new_key, new_value = tuple(
        (jnp.dot(whole, piece, preferred_element_type=jnp.float32) for piece in pieces)
    )
    query = query.astype(jnp.bfloat16)
    new_key = new_key.astype(jnp.bfloat16)
    new_value = new_value.astype(jnp.bfloat16)
    prefix = prefix_cache[0]
    plen = prefix_len[0]
    pre = prefix.shape[1]
    groups = lax.axis_size("group")
    own = owners[:, 0]
    nblk = own.shape[0]
    cap = max(2, 2 * nblk // groups)
    block_len = (pre + rows) // nblk
    onehot = (own[:, None] == jnp.arange(groups, dtype=jnp.int32)[None, :]).astype(jnp.int32)
    rank = jnp.cumsum(onehot, axis=0) - onehot
    slot = own * cap + jnp.sum(rank * onehot, axis=1)
    select = (slot[None, :] == jnp.arange(groups * cap, dtype=jnp.int32)[:, None]).astype(
        jnp.bfloat16
    )
    keep = (jnp.arange(pre) < plen)[None, :, None]
    masked = jnp.where(keep, prefix, jnp.zeros_like(prefix))
    prefix_blocks_local = masked.reshape(2, pre // block_len, block_len, local_width)
    fresh = jnp.stack([new_key, new_value], 0).reshape(2, rows // block_len, block_len, local_width)
    context = attend(query, new_key, new_value, prefix, plen)
    gathered = jnp.dot(
        context,
        lax.all_gather(w_out, "group", axis=1, tiled=True),
        preferred_element_type=jnp.float32,
    )
    attn_out = lax.psum_scatter(
        gathered.astype(jnp.bfloat16), "tensor", scatter_dimension=1, tiled=True
    )
    all_blocks = jnp.concatenate([prefix_blocks_local, fresh], 1)
    send = jnp.einsum(
        "sb,kbtx->sktx", select, all_blocks, preferred_element_type=jnp.float32
    ).astype(jnp.bfloat16)
    received = lax.all_to_all(send, "group", split_axis=0, concat_axis=0, tiled=True)
    decode_cache = received.reshape(1, groups * cap, 2, block_len, local_width)
    return (attn_out, decode_cache)


def solution(mesh):
    in_specs = (
        P("group", "tensor"),
        P("group", "tensor"),
        P("group", "tensor"),
        P("group", "tensor"),
        P("tensor", "group"),
        P("group", None, None, "tensor"),
        P("group"),
        P("group", None),
    )
    out_specs = (P("group", "tensor"), P("group", None, None, None, "tensor"))
    return jax.shard_map(body, mesh=mesh, in_specs=in_specs, out_specs=out_specs, check_vma=False)
```

profile of v0, /device:TPU:24, one launch (start us, length us, event | category | flops | bytes accessed | tf_op | source)
XLA Modules:
  0.0 665.4 jit_solution(1424129424481289707)
XLA Ops:
  7.9 0.7 all-gather.6.cloned.1.call-update
  10.6 0.7 fusion.20
  11.4 0.8 select_reduce_fusion
  12.3 1.2 copy_select_fusion
  14.2 140.0 %all-gather.12.cloned.1.call-done = bf16[2048,256]{1,0:T(8,128)(2,1)} async-done(((bf16[32,256]{1,0:T(8,128)(2,1)}), bf16[2048,256]{1,0:T(8,128)(2,1)}) %all-gather.12.cloned.1.call-update) | async-done | bytes 1048592 | tf_op jit(solution)/shard_map/all_gather | solution.py:36
  154.1 32.4 %all-gather.6.cloned.1.call-done = bf16[512,2048]{1,0:T(8,128)(2,1)} async-done(((bf16[512,256]{1,0:T(8,128)(2,1)}), bf16[512,2048]{1,0:T(8,128)(2,1)}) %all-gather.6.cloned.1.call-update) | async-done | bytes 2097168 | tf_op jit(solution)/shard_map/all_gather | solution.py:31
  186.6 2.6 convolution_convert_fusion.2
  189.2 141.0 %all-gather.8.cloned.1.call-done = bf16[2048,256]{1,0:T(8,128)(2,1)} async-done(((bf16[32,256]{1,0:T(8,128)(2,1)}), bf16[2048,256]{1,0:T(8,128)(2,1)}) %all-gather.8.cloned.1.call-update) | async-done | bytes 1048592 | tf_op jit(solution)/shard_map/all_gather | solution.py:37
  330.3 2.6 convolution_convert_fusion.4
  332.9 0.8 convolution_convert_fusion.1
  333.7 2.5 copy.36
  336.3 10.4 %all-to-all-start = ((bf16[128,2,16,256]{3,2,1,0:T(8,128)(2,1)}), bf16[128,2,16,256]{3,2,1,0:T(8,128)(2,1)S(1)}, u32[]{:S(2)}, u32[]{:S(2)}) async-start(bf16[128,2,16,256]{3,2,1,0:T(8,128)(2,1)} %copy.36), calls=%async_computation.1 | async-start | bytes 4194304 | tf_op jit(solution)/shard_map/all_to_all | solution.py:76
  347.4 0.7 fusion.29
  348.1 1.2 fusion.4
  349.3 1.1 copy.40
  350.9 131.0 %all-gather.10.cloned.1.call-done = bf16[2048,256]{1,0:T(8,128)(2,1)} async-done(((bf16[32,256]{1,0:T(8,128)(2,1)}), bf16[2048,256]{1,0:T(8,128)(2,1)}) %all-gather.10.cloned.1.call-update) | async-done | bytes 1048592 | tf_op jit(solution)/shard_map/all_gather | solution.py:35
  481.9 2.6 convolution_convert_fusion.3
  484.5 0.8 fusion.16
  485.6 2.0 fusion.30
  487.6 0.9 fusion.7
  488.5 131.3 %all-gather.14.cloned.1.call-done = bf16[256,2048]{0,1:T(8,128)(2,1)} async-done(((bf16[256,32]{0,1:T(8,128)(2,1)}), bf16[256,2048]{0,1:T(8,128)(2,1)}) %all-gather.14.cloned.1.call-update) | async-done | bytes 1048592 | tf_op jit(solution)/shard_map/all_gather | solution.py:66
  619.7 3.3 convolution_convert_fusion
  623.1 34.2 %reduce-scatter.2.cloned.1.call-done = bf16[512,256]{1,0:T(8,128)(2,1)} async-done(((bf16[512,2048]{1,0:T(8,128)(2,1)}), bf16[512,256]{1,0:T(8,128)(2,1)}) %reduce-scatter.2.cloned.1.call-update) | async-done | bytes 262160 | tf_op jit(solution)/shard_map/reduce_scatter | solution.py:69
  657.3 1.3 copy.46
  (27 shorter events, 4.4 us)
Async XLA Ops:
  7.2 147.0 %all-gather.12.cloned.1.call-start = ((), (), s32[]{:S(2)}) async-start(), calls=%async_computation.5 | async-start | bytes 1064960 | tf_op jit(solution)/shard_map/all_gather | solution.py:36
  7.9 178.7 %all-gather.6.cloned.1.call-start = ((), (), s32[]{:S(2)}) async-start(), calls=%async_computation.2 | async-start | bytes 2359296 | tf_op jit(solution)/shard_map/all_gather | solution.py:31
  8.6 321.6 %all-gather.8.cloned.1.call-start = ((), (), s32[]{:S(2)}) async-start(), calls=%async_computation.3 | async-start | bytes 1064960 | tf_op jit(solution)/shard_map/all_gather | solution.py:37
  9.4 472.5 %all-gather.10.cloned.1.call-start = ((), (), s32[]{:S(2)}) async-start(), calls=%async_computation.4 | async-start | bytes 1064960 | tf_op jit(solution)/shard_map/all_gather | solution.py:35
  336.3 11.1 %copy-start = (bf16[1,2,512,256]{3,2,1,0:T(8,128)(2,1)S(1)}, bf16[1,2,512,256]{3,2,1,0:T(8,128)(2,1)}, u32[]{:S(2)}) copy-start(bf16[1,2,512,256]{3,2,1,0:T(8,128)(2,1)} %param.13) | copy-start | bytes 1572868
  336.3 286.8 %all-to-all-start = ((bf16[128,2,16,256]{3,2,1,0:T(8,128)(2,1)}), bf16[128,2,16,256]{3,2,1,0:T(8,128)(2,1)S(1)}, u32[]{:S(2)}, u32[]{:S(2)}) async-start(bf16[128,2,16,256]{3,2,1,0:T(8,128)(2,1)} %copy.36), calls=%async_computation.1 | async-start | bytes 4194304 | tf_op jit(solution)/shard_map/all_to_all | solution.py:76
  346.7 273.0 %all-gather.14.cloned.1.call-start = ((), (), s32[]{:S(2)}) async-start(), calls=%async_computation.6 | async-start | bytes 1064960 | tf_op jit(solution)/shard_map/all_gather | solution.py:66
  347.3 310.0 %reduce-scatter.2.cloned.1.call-start = ((), (), s32[]{:S(2)}) async-start(), calls=%async_computation.7 | async-start | bytes 2359296 | tf_op jit(solution)/shard_map/reduce_scatter | solution.py:69
  484.5 1.0 copy-start.1
Sparse Core Ops, SparseCore 0:
  10.9 143.1 all-gather.11
  156.2 30.2 all-gather.5
  189.5 140.6 all-gather.7
  333.1 148.8 all-gather.9
  484.7 134.9 all-gather.13
  623.2 34.0 reduce-scatter.1
where the time goes:
time: 669 us; the launch traced here: 665 us
  waiting for transfers between devices  613 us (92%)
  between operations  14.9 us (2%)
  matrix products  13.5 us (2%)
  starting transfers between devices  10.7 us (2%)
  other arithmetic  6.71 us (1%)
    all_gather x1, waiting for transfers between devices, body(): lax.all_gather(w_value, 'group', axis=0, tiled=True)  141 us
    all_gather x1, waiting for transfers between devices, body(): lax.all_gather(w_key, 'group', axis=0, tiled=True)  140 us
    all_gather x1, waiting for transfers between devices, body(): lax.all_gather(w_out, 'group', axis=1, tiled=True)  131 us
    all_gather x1, waiting for transfers between devices, body(): lax.all_gather(w_query, 'group', axis=0, tiled=True)  131 us
    reduce_scatter x1, waiting for transfers between devices, body(): lax.psum_scatter(gathered.astype(jnp.bfloat16), 'tensor', scatter_dimensi...  34.2 us
    all_gather x1, waiting for transfers between devices, body(): whole = lax.all_gather(tokens, 'tensor', axis=1, tiled=True)  32.4 us
  transfers between devices with their start and end apart: 7, of which 6 were waited for; matrix products, arithmetic and copies ran while one was open for 4% of the time, Pallas kernels for 0%

commit v1 on v0

v1 whole, which is shorter than its diff:
```python
import functools

import jax
import jax.numpy as jnp
from jax import lax
from jax.experimental import pallas as pl
from jax.experimental.pallas import tpu as pltpu
from jax.sharding import PartitionSpec as P

HD = 128
NX = 4
NC = 2
JUMP = 2
MESH = pl.DeviceIdType.MESH


def gather_kernel(nz, ny, nw, *refs):
    w_refs, tok_ref, w_out, tok_out = refs[:nw], refs[nw], refs[nw + 1], refs[nw + 2]
    zs, zr, xs, xr, ds, dr, loc, ts, tr = refs[nw + 3 :]
    g, t = lax.axis_index("group"), lax.axis_index("tensor")
    z, x = g // NX, g % NX
    y, c = t // NC, t % NC
    depth = w_refs[0].shape[0]
    half, width = tok_ref.shape[0] // 2, tok_ref.shape[1]
    up, down = nz // 2, (nz - 1) // 2

    def at_z(step):
        return ((z + step + nz) % nz * NX + x, t)

    def at_x(step):
        return (z * NX + (x + step + NX) % NX, t)

    def at_y(step):
        return (g, (y + step + ny) % ny * NC + c)

    sibling = (g, y * NC + (1 - c))

    mine = pl.ds(pl.multiple_of(g * depth, depth), depth)
    own_copies = [
        pltpu.make_async_copy(ref, w_out.at[i, mine, :], loc.at[i])
        for i, ref in enumerate(w_refs)
    ]
    own_copies.append(
        pltpu.make_async_copy(
            tok_ref, tok_out.at[:, pl.ds(pl.multiple_of(t * width, width), width)], loc.at[nw]
        )
    )
    for copy in own_copies:
        copy.start()

    peers = [at_z(j) for j in range(1, JUMP + 1)] + [at_z(-j) for j in range(1, JUMP + 1)]
    peers += [at_x(1), at_x(-1), at_y(1), at_y(-1), sibling]
    barrier = pltpu.get_barrier_semaphore()
    for peer in peers:
        pl.semaphore_signal(barrier, inc=1, device_id=peer, device_id_type=MESH)
    for copy in own_copies:
        copy.wait()
    pl.semaphore_wait(barrier, len(peers))

    started = []

    def send(src, dst, ssem, rsem, peer):
        copy = pltpu.make_async_remote_copy(
            src_ref=src, dst_ref=dst, send_sem=ssem, recv_sem=rsem,
            device_id=peer, device_id_type=MESH,
        )
        copy.start()
        started.append(copy)

    def arrived(dst, rsem):
        pltpu.make_async_copy(dst, dst, rsem).wait()

    def z_of(k):
        return (z - k + nz) % nz if k <= up else (z + (k - up)) % nz

    def rows(k, step_x):
        owner = z_of(k) * NX + (x + step_x + NX) % NX
        return w_out.at[:, pl.ds(pl.multiple_of(owner * depth, depth), depth), :]

    def along_z(k, d, sign, most):
        src = rows(k, 0)
        for j in range(min(JUMP, most - d), 0, -1):
            kk = (d + j) if sign > 0 else up + d + j
            send(src, rows(k, 0), zs.at[kk], zr.at[kk], at_z(sign * j))

    def along_x(k):
        src = rows(k, 0)
        send(src, rows(k, 0), xs.at[0, k], xr.at[0, k], at_x(1))
        send(src, rows(k, 0), xs.at[1, k], xr.at[1, k], at_x(-1))

    def across_x(k):
        arrived(rows(k, -1), xr.at[0, k])
        arrived(rows(k, 1), xr.at[1, k])
        if k % 2 == 0:
            send(rows(k, -1), rows(k, -1), ds.at[k], dr.at[k], at_x(1))
        else:
            send(rows(k, 1), rows(k, 1), ds.at[k], dr.at[k], at_x(-1))

    def tokens(step_y, h, core):
        owner = (y + step_y + ny) % ny * NC + core
        return tok_out.at[
            pl.ds(h * half, half), pl.ds(pl.multiple_of(owner * width, width), width)
        ]

    def to_sibling(step_y, h, n):
        send(tokens(step_y, h, c), tokens(step_y, h, c), ts.at[n], tr.at[n], sibling)

    along_z(0, 0, 1, up)
    along_z(0, 0, -1, down)
    along_x(0)
    for h in range(2):
        send(tokens(0, h, c), tokens(0, h, c), ts.at[h], tr.at[h], at_y(1))
        send(tokens(0, 1 - h, c), tokens(0, 1 - h, c), ts.at[3 - h], tr.at[3 - h], at_y(-1))
    for h in range(2):
        to_sibling(0, h, 6 + h)

    def token_step(n):
        if n == 0:
            arrived(tokens(-1, 0, c), tr.at[0])
            send(tokens(-1, 0, c), tokens(-1, 0, c), ts.at[4], tr.at[4], at_y(1))
            to_sibling(-1, 0, 8)
            arrived(tokens(1, 1, c), tr.at[3])
            send(tokens(1, 1, c), tokens(1, 1, c), ts.at[5], tr.at[5], at_y(-1))
            to_sibling(1, 1, 11)
        elif n == 1:
            arrived(tokens(-1, 1, c), tr.at[1])
            to_sibling(-1, 1, 9)
            arrived(tokens(1, 0, c), tr.at[2])
            to_sibling(1, 0, 10)
        else:
            for h in range(2):
                arrived(tokens(2, h, c), tr.at[4 + h])
                to_sibling(2, h, 12 + h)

    behind = [0]
    for d in range(1, up + 1):
        ahead = []
        for sign, most in ((1, up), (-1, down)):
            if d > most:
                continue
            k = d if sign > 0 else up + d
            arrived(rows(k, 0), zr.at[k])
            if d % JUMP == 0 and d < most:
                along_z(k, d, sign, most)
            along_x(k)
            ahead.append(k)
        for k in behind:
            across_x(k)
        behind = ahead
        if d in (up // 2 - 1, up // 2 + 1, up - 1):
            token_step((up // 2 - 1, up // 2 + 1, up - 1).index(d))
    for k in behind:
        across_x(k)
    for k in range(nz):
        arrived(rows(k, 2), dr.at[k])
    for n, step_y in enumerate((0, 0, -1, -1, 1, 1, 2, 2)):
        arrived(tokens(step_y, n % 2, 1 - c), tr.at[6 + n])
    for copy in started:
        copy.wait_send()


def gather(ws, tok, nz, ny):
    nw = len(ws)
    depth, cols = ws[0].shape
    vmem, hbm = pl.BlockSpec(memory_space=pltpu.VMEM), pl.BlockSpec(memory_space=pl.ANY)
    dma = pltpu.SemaphoreType.DMA
    sent = (nz - 1 + 3 * nz) * nw * ws[0].size * 2 + 7 * tok.size * 2
    return pl.pallas_call(
        functools.partial(gather_kernel, nz, ny, nw),
        out_shape=[
            jax.ShapeDtypeStruct((nw, depth * nz * NX, cols), tok.dtype),
            jax.ShapeDtypeStruct((tok.shape[0], tok.shape[1] * ny * NC), tok.dtype),
        ],
        in_specs=[hbm] * (nw + 1),
        out_specs=[vmem] * 2,
        scratch_shapes=[
            dma((nz,)), dma((nz,)), dma((2, nz)), dma((2, nz)), dma((nz,)), dma((nz,)),
            dma((nw + 1,)), dma((14,)), dma((14,)),
        ],
        compiler_params=pltpu.CompilerParams(
            collective_id=0, has_side_effects=True, vmem_limit_bytes=24 << 20
        ),
        cost_estimate=pl.CostEstimate(flops=0, bytes_accessed=2 * sent, transcendentals=0),
    )(*ws, tok)


def pack_kernel(groups, cap, own_ref, plen_ref, tok_ref, w_ref, pre_ref, fresh_ref, send_ref, count):
    pre = pre_ref.shape[1]
    block = send_ref.shape[2]
    pre_blocks = pre // block
    nblk = own_ref.shape[0]
    send_ref[...] = jnp.zeros_like(send_ref)
    for kind in range(2):
        fresh_ref[kind] = jnp.dot(
            tok_ref[...], w_ref[kind], preferred_element_type=jnp.float32
        ).astype(fresh_ref.dtype)

    @pl.loop(0, groups)
    def _(i):
        count[i] = 0

    def slot_of(b):
        owner = own_ref[b, 0]
        rank = count[owner]
        count[owner] = rank + 1
        return owner * cap + rank

    plen = plen_ref[0]

    @pl.loop(0, pre_blocks)
    def _(b):
        slot = slot_of(b)
        row = pl.multiple_of(b * block, block)
        kept = lax.broadcasted_iota(jnp.int32, (block, pre_ref.shape[2]), 0) + row < plen
        for kind in range(2):
            rows = pre_ref[kind, pl.ds(row, block), :]
            send_ref[slot, kind] = jnp.where(kept, rows, jnp.zeros_like(rows))

    @pl.loop(0, nblk - pre_blocks)
    def _(b):
        slot = slot_of(b + pre_blocks)
        row = pl.multiple_of(b * block, block)
        for kind in range(2):
            send_ref[slot, kind] = fresh_ref[kind, pl.ds(row, block), :]


def pack(owners, prefix_len, tokens, w, prefix, groups, cap):
    nblk = owners.shape[0]
    rows, width = tokens.shape[0], prefix.shape[2]
    block = (prefix.shape[1] + rows) // nblk
    vmem = pl.BlockSpec(memory_space=pltpu.VMEM)
    smem = pl.BlockSpec(memory_space=pltpu.SMEM)
    return pl.pallas_call(
        functools.partial(pack_kernel, groups, cap),
        out_shape=[
            jax.ShapeDtypeStruct((2, rows, width), tokens.dtype),
            jax.ShapeDtypeStruct((groups * cap, 2, block, width), tokens.dtype),
        ],
        in_specs=[smem, smem, vmem, vmem, vmem],
        out_specs=[vmem, vmem],
        scratch_shapes=[pltpu.SMEM((groups,), jnp.int32)],
        compiler_params=pltpu.CompilerParams(vmem_limit_bytes=32 << 20),
        cost_estimate=pl.CostEstimate(
            flops=4 * rows * tokens.shape[1] * width, bytes_accessed=8 << 20, transcendentals=0
        ),
    )(owners, prefix_len, tokens, w, prefix)


def attend(query, new_key, new_value, prefix, plen):
    rows, width = query.shape
    heads = width // HD
    pre = prefix.shape[1]
    keys = jnp.concatenate([prefix[0], new_key], 0).reshape(pre + rows, heads, HD)
    values = jnp.concatenate([prefix[1], new_value], 0).reshape(pre + rows, heads, HD)
    qmat = query.reshape(rows, heads, HD)
    scores = jnp.einsum("chd,khd->hck", qmat, keys, preferred_element_type=jnp.float32) * HD ** (
        -0.5
    )
    kpos = jnp.arange(pre + rows)[None, :]
    cpos = jnp.arange(rows)[:, None]
    valid = jnp.where(kpos < pre, kpos < plen, kpos - pre <= cpos)
    scores = jnp.where(valid[None], scores, -jnp.inf)
    top = jnp.max(scores, axis=-1, keepdims=True)
    expo = jnp.exp(scores - top)
    weights = (expo / jnp.sum(expo, axis=-1, keepdims=True)).astype(jnp.bfloat16)
    context = jnp.einsum("hck,khd->chd", weights, values, preferred_element_type=jnp.float32)
    return context.astype(jnp.bfloat16).reshape(rows, width)


def body(tokens, w_query, w_key, w_value, w_out, prefix_cache, prefix_len, owners):
    groups, tensors = lax.axis_size("group"), lax.axis_size("tensor")
    nz, ny = groups // NX, tensors // NC
    w_all, whole = gather((w_key, w_value, w_query, w_out.T), tokens, nz, ny)
    prefix = prefix_cache[0]
    cap = max(2, 2 * owners.shape[0] // groups)
    fresh, send = pack(owners, prefix_len, whole, w_all, prefix, groups, cap)
    received = lax.all_to_all(send, "group", split_axis=0, concat_axis=0, tiled=True)
    decode_cache = received[None]
    query = jnp.dot(whole, w_all[2], preferred_element_type=jnp.float32).astype(jnp.bfloat16)
    context = attend(query, fresh[0], fresh[1], prefix, prefix_len[0])
    gathered = lax.dot_general(
        context, w_all[3], (((1,), (1,)), ((), ())), preferred_element_type=jnp.float32
    )
    attn_out = lax.psum_scatter(
        gathered.astype(jnp.bfloat16), "tensor", scatter_dimension=1, tiled=True
    )
    return (attn_out, decode_cache)


def solution(mesh):
    in_specs = (
        P("group", "tensor"),
        P("group", "tensor"),
        P("group", "tensor"),
        P("group", "tensor"),
        P("tensor", "group"),
        P("group", None, None, "tensor"),
        P("group"),
        P("group", None),
    )
    out_specs = (P("group", "tensor"), P("group", None, None, None, "tensor"))
    return jax.shard_map(body, mesh=mesh, in_specs=in_specs, out_specs=out_specs, check_vma=False)
```

time: 669 us -> 194 us (0.29)
  waiting for transfers between devices: 613 us -> 85.5 us
  Pallas kernels: 0 us -> 60.6 us
  local copies, waits for them, and re-layouts: 6.58 us -> 13.8 us
    all_gather x5 -> x0, waiting for transfers between devices: 576 us -> none  [the longest x1 141 us: body(): lax.all_gather(w_value, 'group', axis=0, tiled=True)]
    all_to_all x1, waiting for transfers between devices: 0.01 us -> 85.5 us  [body(): lax.all_to_all(send, 'group', split_axis=0, concat_axis=0, tiled=True)]
    pallas_call x0 -> x2, Pallas kernels: none -> 60.6 us  [the longest x1 55.9 us: gather(): pl.pallas_call(functools.partial(gather_kernel, nz, ny, nw), out_shape=[j...]
    reduce_scatter x1, waiting for transfers between devices: 34.2 us -> 0.01 us  [body(): lax.psum_scatter(gathered.astype(jnp.bfloat16), 'tensor', scatter_dimensi...]
    unnamed x6 -> x21, local copies, waits for them, and re-layouts: 2.69 us -> 10.8 us
  transfers between devices with their start and end apart: 7 -> 2, of which waited for: 6 -> 1; matrix products, arithmetic and copies ran while one was open for 4% -> 6% of each run, Pallas kernels for 0% -> 0%
where the time goes in v1:
time: 194 us; the launch traced here: 193 us
  waiting for transfers between devices  85.5 us (44%)
  Pallas kernels  60.6 us (31%)
  between operations  14.8 us (8%)
  local copies, waits for them, and re-layouts  13.8 us (7%)
  starting transfers between devices  9.08 us (5%)
  matrix products  6.98 us (4%)
  other arithmetic  2.37 us (1%)
    all_to_all x1, waiting for transfers between devices, body(): lax.all_to_all(send, 'group', split_axis=0, concat_axis=0, tiled=True)  85.5 us
    pallas_call x1, Pallas kernels, gather(): pl.pallas_call(functools.partial(gather_kernel, nz, ny, nw), out_shape=[j...  55.9 us
    unnamed x21, local copies, waits for them, and re-layouts  10.8 us
    all_to_all x1, starting transfers between devices, body(): lax.all_to_all(send, 'group', split_axis=0, concat_axis=0, tiled=True)  9.04 us
    pallas_call x1, Pallas kernels, pack(): pl.pallas_call(functools.partial(pack_kernel, groups, cap), out_shape=[ja...  4.76 us
  transfers between devices with their start and end apart: 2, of which 1 were waited for; matrix products, arithmetic and copies ran while one was open for 6% of the time, Pallas kernels for 0%

profile of v1, /device:TPU:24, one launch (start us, length us, event | category | flops | bytes accessed | tf_op | source)
XLA Modules:
  0.0 193.1 jit_solution(7073322539583408152)
XLA Ops:
  7.8 0.7 copy.16.own_ref
  8.6 0.9 copy-done.3
  9.5 0.7 copy-done.4
  10.2 0.7 copy-done.5
  10.9 0.7 copy-done.6
  11.7 0.7 copy-done.7
  12.4 55.9 %shard_map.95 = (bf16[4,2048,256]{2,1,0:T(8,128)(2,1)S(1)}, bf16[512,2048]{1,0:T(8,128)(2,1)S(1)}) custom-call(bf16[32,256]{1,0:T(8,128)(2,1)S(1)} %copy-done.4, bf16[32,256]{1,0:T(8,128)(2,1)S(1)} %copy-done.5, bf16[32,256]{1,0:T(8,128)(2,1)S(1)} %copy-done.6, bf16[32,256]{1,0:T(8,128)(2,1)S(1)} %bitcast.22, bf16[512,256]{1,0:T(8,128)(2,1)S(1)} %copy-done.3), custom_call_target="tpu_custom_call" | custom-call | bytes 11927552 | tf_op jit(solution)/shard_map/pallas_call | solution.py:168
  68.3 1.0 copy-done.1
  69.3 4.8 %shard_map.96 = (bf16[2,512,256]{2,1,0:T(8,128)(2,1)S(1)}, bf16[128,2,16,256]{3,2,1,0:T(8,128)(2,1)}) custom-call(s32[64,1]{1,0:T(8,128)S(1)} %copy.16.own_ref, s32[1]{0:T(128)} %copy.26.plen_ref, bf16[512,2048]{1,0:T(8,128)(2,1)S(1)} %get-tuple-element.6.tok_ref, bf16[4,2048,256]{2,1,0:T(8,128)(2,1)S(1)} %get-tuple-element.7.w_ref, ...), custom_call_target="tpu_custom_call" | custom-call | flops 1073741824 | bytes 8388608 | tf_op jit(solution)/shard_map/pallas_call | solution.py:233
  74.1 1.9 %copy-done = bf16[4,2048,256]{2,1,0:T(8,128)(2,1)} copy-done((bf16[4,2048,256]{2,1,0:T(8,128)(2,1)}, bf16[4,2048,256]{2,1,0:T(8,128)(2,1)S(1)}, u32[]{:S(2)}) %copy-start) | copy-done | bytes 4194328
  76.0 9.0 %all-to-all-start = ((bf16[128,2,16,256]{3,2,1,0:T(8,128)(2,1)}), bf16[128,2,16,256]{3,2,1,0:T(8,128)(2,1)}, u32[]{:S(2)}, u32[]{:S(2)}) async-start(bf16[128,2,16,256]{3,2,1,0:T(8,128)(2,1)} %get-tuple-element.9), calls=%async_computation.1 | async-start | bytes 4194304 | tf_op jit(solution)/shard_map/all_to_all | solution.py:277
  85.1 0.7 fusion.23
  85.9 1.8 copy.15
  87.7 0.1 copy.24
  87.8 0.2 copy.19
  88.0 0.1 copy.23
  88.3 0.4 fusion.4
  88.7 2.0 %convolution_convert_fusion.1 = bf16[512,256]{0,1:T(8,128)(2,1)S(1)} fusion(bf16[512,2048]{1,0:T(8,128)(2,1)S(1)} %get-tuple-element.6.tok_ref, bf16[4,2048,256]{2,1,0:T(8,128)(2,1)} %copy-done), kind=kOutput, calls=%fused_computation.13 | convolution fusion | flops 537001984 | bytes 3407872 | tf_op jit(solution)/shard_map/dot_general | solution.py:279
  90.7 0.8 fusion.15
  91.5 2.0 %fusion.25 = (f32[2,512]{1,0:T(2,128)S(1)}, f32[2,512,1024]{2,1,0:T(8,128)S(1)}) fusion(f32[2,512,1024]{2,1,0:T(8,128)S(1)} %fusion.15, pred[512,1024]{1,0:T(8,128)(4,1)S(1)} %fusion.4), kind=kOutput, calls=%fused_computation.34 | output fusion | flops 6292479 | bytes 8916992 | tf_op jit(solution)/shard_map/sub | solution.py:264
  93.4 0.9 fusion.7
  94.4 3.3 %convolution_convert_fusion = bf16[512,2048]{1,0:T(8,128)(2,1)} fusion(bf16[512,256]{0,1:T(8,128)(2,1)S(1)} %bitcast.27, bf16[4,2048,256]{2,1,0:T(8,128)(2,1)} %copy-done), kind=kOutput, calls=%fused_computation.5 | convolution fusion | flops 537919488 | bytes 3407872 | tf_op jit(solution)/shard_map/dot_general | solution.py:281
  97.7 85.5 %all-to-all-done = bf16[128,2,16,256]{3,2,1,0:T(8,128)(2,1)} async-done(((bf16[128,2,16,256]{3,2,1,0:T(8,128)(2,1)}), bf16[128,2,16,256]{3,2,1,0:T(8,128)(2,1)}, u32[]{:S(2)}, u32[]{:S(2)}) %all-to-all-start) | async-done | bytes 2097184 | tf_op jit(solution)/shard_map/all_to_all | solution.py:277
  183.2 3.1 %copy.27 = bf16[1,128,2,16,256]{4,3,2,1,0:T(8,128)(2,1)} copy(bf16[1,128,2,16,256]{4,3,2,1,0:T(8,128)(2,1)} %bitcast.11) | data formatting | bytes 4194304
  (20 shorter events, 0.2 us)
Async XLA Ops:
  8.6 0.9 copy-start.3
  9.5 0.7 copy-start.4
  10.2 0.7 copy-start.5
  10.9 0.7 copy-start.6
  11.7 0.7 copy-start.7
  68.2 1.0 copy-start.1
  69.3 15.8 %copy-start.2 = (bf16[1,2,512,256]{3,2,1,0:T(8,128)(2,1)S(1)}, bf16[1,2,512,256]{3,2,1,0:T(8,128)(2,1)}, u32[]{:S(2)}) copy-start(bf16[1,2,512,256]{3,2,1,0:T(8,128)(2,1)} %param.13) | copy-start | bytes 1572868
  74.1 1.9 %copy-start = (bf16[4,2048,256]{2,1,0:T(8,128)(2,1)}, bf16[4,2048,256]{2,1,0:T(8,128)(2,1)S(1)}, u32[]{:S(2)}) copy-start(bf16[4,2048,256]{2,1,0:T(8,128)(2,1)S(1)} %get-tuple-element.7.w_ref) | copy-start | bytes 12582916
  76.0 107.2 %all-to-all-start = ((bf16[128,2,16,256]{3,2,1,0:T(8,128)(2,1)}), bf16[128,2,16,256]{3,2,1,0:T(8,128)(2,1)}, u32[]{:S(2)}, u32[]{:S(2)}) async-start(bf16[128,2,16,256]{3,2,1,0:T(8,128)(2,1)} %get-tuple-element.9), calls=%async_computation.1 | async-start | bytes 4194304 | tf_op jit(solution)/shard_map/all_to_all | solution.py:277
  85.1 98.2 %reduce-scatter.2.cloned.1.call-start = ((), (), s32[]{:S(2)}) async-start(), calls=%async_computation.2 | async-start | bytes 2359296 | tf_op jit(solution)/shard_map/reduce_scatter | solution.py:284
  91.4 2.0 %copy-start.8 = (bf16[1,1,512,256]{2,3,1,0:T(8,128)(2,1)S(1)}, bf16[1,1,512,256]{2,3,1,0:T(8,128)(2,1)}, u32[]{:S(2)}) copy-start(bf16[1,1,512,256]{2,3,1,0:T(8,128)(2,1)} %copy.15) | copy-start | bytes 786436
Sparse Core Ops, SparseCore 0:
  97.8 39.5 reduce-scatter.1

commit v2 on v1

v2 whole, which is shorter than its diff:
```python
import functools

import jax
import jax.numpy as jnp
from jax import lax
from jax.experimental import pallas as pl
from jax.experimental.pallas import tpu as pltpu
from jax.sharding import PartitionSpec as P

HD = 128
NX = 4
NC = 2
JUMP = 2
TILE = 128
MESH = pl.DeviceIdType.MESH
BF16, F32 = jnp.bfloat16, jnp.float32


def kernel(nz, ny, cap, *refs):
    w_refs, tok_ref, pre_ref, plen_ref, own_ref = refs[:4], refs[4], refs[5], refs[6], refs[7]
    attn_out, cache_out = refs[8:10]
    w, tok, pre, cache, packed, where_v, where_s, query, context = refs[10:19]
    mine, sib_send, sib_recv, y_send, y_recv = refs[19:24]
    zs, zr, qzs, qzr, xs, xr, ds, dr, qxs, qxr, ts, tr, loc, bs, br, ys, yr, ex = refs[24:]

    g, t = lax.axis_index("group"), lax.axis_index("tensor")
    z, x = g // NX, g % NX
    y, c = t // NC, t % NC
    groups = nz * NX
    rows_n, width = tok_ref.shape
    half = rows_n // 2
    pre_n = pre_ref.shape[2]
    nblk = own_ref.shape[0]
    block = (pre_n + rows_n) // nblk
    up, down = nz // 2, (nz - 1) // 2

    def at_z(step):
        return ((z + step + nz) % nz * NX + x, t)

    def at_x(step):
        return (z * NX + (x + step + NX) % NX, t)

    def at_y(step):
        return (g, (y + step + ny) % ny * NC + c)

    sibling = (g, y * NC + (1 - c))

    own_copies = [
        pltpu.make_async_copy(ref, w.at[i, z, x], loc.at[i]) for i, ref in enumerate(w_refs)
    ]
    own_copies.append(
        pltpu.make_async_copy(
            tok_ref, tok.at[:, pl.ds(pl.multiple_of(t * width, width), width)], loc.at[4]
        )
    )
    own_pre = pltpu.make_async_copy(pre_ref.at[0], pre, loc.at[5])
    for copy in own_copies + [own_pre]:
        copy.start()

    barrier = pltpu.get_barrier_semaphore()

    @pl.loop(1, groups)
    def _(i):
        pl.semaphore_signal(barrier, inc=1, device_id=((g + i) % groups, t), device_id_type=MESH)

    for peer in [at_y(i) for i in range(1, ny)] + [sibling]:
        pl.semaphore_signal(barrier, inc=1, device_id=peer, device_id_type=MESH)
    for copy in own_copies:
        copy.wait()
    pl.semaphore_wait(barrier, groups - 1 + ny)

    started = []

    def send(src, dst, ssem, rsem, peer):
        copy = pltpu.make_async_remote_copy(
            src_ref=src, dst_ref=dst, send_sem=ssem, recv_sem=rsem,
            device_id=peer, device_id_type=MESH,
        )
        copy.start()
        started.append(copy)

    def arrived(dst, rsem):
        pltpu.make_async_copy(dst, dst, rsem).wait()

    def z_of(k):
        return (z - k + nz) % nz if k <= up else (z + (k - up)) % nz

    def kv(k, step_x):
        return w.at[pl.ds(0, 2), z_of(k), (x + step_x + NX) % NX]

    def qo(k):
        return w.at[pl.ds(2, 2), z_of(k), x]

    def along_z(item, k, d, sign, most, ssem, rsem):
        for j in range(min(JUMP, most - d), 0, -1):
            kk = (d + j) if sign > 0 else up + d + j
            send(item(k), item(k), ssem.at[kk], rsem.at[kk], at_z(sign * j))

    def kv_here(k):
        return kv(k, 0)

    def along_x(k):
        send(kv(k, 0), kv(k, 0), xs.at[0, k], xr.at[0, k], at_x(1))
        send(kv(k, 0), kv(k, 0), xs.at[1, k], xr.at[1, k], at_x(-1))

    def across_x(k):
        arrived(kv(k, -1), xr.at[0, k])
        arrived(kv(k, 1), xr.at[1, k])
        if k % 2 == 0:
            send(kv(k, -1), kv(k, -1), ds.at[k], dr.at[k], at_x(1))
        else:
            send(kv(k, 1), kv(k, 1), ds.at[k], dr.at[k], at_x(-1))

    def tokens(step_y, h, core):
        owner = (y + step_y + ny) % ny * NC + core
        return tok.at[pl.ds(h * half, half), pl.ds(pl.multiple_of(owner * width, width), width)]

    def to_sibling(step_y, h, n):
        send(tokens(step_y, h, c), tokens(step_y, h, c), ts.at[n], tr.at[n], sibling)

    for sign, most in ((1, up), (-1, down)):
        along_z(kv_here, 0, 0, sign, most, zs, zr)
    along_x(0)
    for h in range(2):
        send(tokens(0, h, c), tokens(0, h, c), ts.at[h], tr.at[h], at_y(1))
        send(tokens(0, 1 - h, c), tokens(0, 1 - h, c), ts.at[3 - h], tr.at[3 - h], at_y(-1))
    for sign, most in ((1, up), (-1, down)):
        along_z(qo, 0, 0, sign, most, qzs, qzr)
    for h in range(2):
        to_sibling(0, h, 6 + h)

    owner_col = own_ref[...]
    bi = lax.broadcasted_iota(jnp.int32, (nblk, nblk), 0)
    bj = lax.broadcasted_iota(jnp.int32, (nblk, nblk), 1)
    owner_row = jnp.sum(jnp.where(bi == bj, owner_col, 0), axis=0, keepdims=True)
    rank = jnp.sum(
        jnp.where((owner_col == owner_row) & (bj < bi), 1, 0), axis=1, keepdims=True
    )
    slot = owner_col * cap + rank
    si = lax.broadcasted_iota(jnp.int32, (nblk, groups * cap), 1)
    sb = lax.broadcasted_iota(jnp.int32, (nblk, groups * cap), 0)
    where_v[...] = nblk - jnp.sum(jnp.where(slot == si, nblk - sb, 0), axis=0, keepdims=True)
    slots = pltpu.make_async_copy(where_v, where_s, loc.at[6])
    slots.start()

    own_pre.wait()
    plen = plen_ref[0]
    filled = lax.broadcasted_iota(jnp.int32, (pre_n, width), 0) < plen
    for kind in range(2):
        rows = pre[kind]
        cache[kind, pl.ds(0, pre_n // block)] = jnp.where(
            filled, rows, jnp.zeros_like(rows)
        ).reshape(pre_n // block, block, width)
        cache[kind, nblk] = jnp.zeros((block, width), cache.dtype)
    slots.wait()

    def token_step(n):
        if n == 0:
            arrived(tokens(-1, 0, c), tr.at[0])
            send(tokens(-1, 0, c), tokens(-1, 0, c), ts.at[4], tr.at[4], at_y(1))
            to_sibling(-1, 0, 8)
            arrived(tokens(1, 1, c), tr.at[3])
            send(tokens(1, 1, c), tokens(1, 1, c), ts.at[5], tr.at[5], at_y(-1))
            to_sibling(1, 1, 11)
        elif n == 1:
            arrived(tokens(-1, 1, c), tr.at[1])
            to_sibling(-1, 1, 9)
            arrived(tokens(1, 0, c), tr.at[2])
            to_sibling(1, 0, 10)
        else:
            for h in range(2):
                arrived(tokens(2, h, c), tr.at[4 + h])
                to_sibling(2, h, 12 + h)

    behind = [(0, 0, 1, 0)]
    token_at = (up // 2 - 1, up // 2 + 1, up - 1)
    for d in range(1, up + 2):
        ahead = []
        for sign, most in ((1, up), (-1, down)):
            if d > most:
                continue
            k = d if sign > 0 else up + d
            arrived(kv(k, 0), zr.at[k])
            if d % JUMP == 0 and d < most:
                along_z(kv_here, k, d, sign, most, zs, zr)
            along_x(k)
            ahead.append((k, d, sign, most))
        for k, dd, sign, most in behind:
            across_x(k)
            if k:
                arrived(qo(k), qzr.at[k])
                if dd % JUMP == 0 and dd < most:
                    along_z(qo, k, dd, sign, most, qzs, qzr)
        behind = ahead
        if d in token_at:
            token_step(token_at.index(d))

    for n, step in enumerate((1, -1, 2)):
        ref = w.at[pl.ds(2, 2), :, x]
        send(ref, ref, qxs.at[n], qxr.at[n], at_x(step))
    for k in range(nz):
        arrived(kv(k, 2), dr.at[k])
    for n, step_y in enumerate((0, 0, -1, -1, 1, 1, 2, 2)):
        arrived(tokens(step_y, n % 2, 1 - c), tr.at[6 + n])

    def project(i):
        return jnp.dot(
            tok[...], w[i].reshape(tok.shape[1], width), preferred_element_type=F32
        ).astype(BF16)

    for kind in range(2):
        cache[kind, pl.ds(pre_n // block, rows_n // block)] = project(kind).reshape(
            rows_n // block, block, width
        )

    @pl.loop(0, groups * cap)
    def _(s):
        b = where_s[0, s]
        for kind in range(2):
            packed[s, kind] = cache[kind, b]

    def exchange(step_z, step_x):
        peer = (z + step_z) % nz * NX + (x + step_x) % NX
        return pltpu.make_async_remote_copy(
            src_ref=packed.at[pl.ds(peer * cap, cap)],
            dst_ref=cache_out.at[pl.ds(g * cap, cap)],
            send_sem=ex.at[0], recv_sem=ex.at[1],
            device_id=(peer, t), device_id_type=MESH,
        )

    keep = pltpu.make_async_copy(
        packed.at[pl.ds(g * cap, cap)], cache_out.at[pl.ds(g * cap, cap)], loc.at[7]
    )
    keep.start()
    for step_x in (0, 1, 3, 2):

        @pl.loop(1, nz + (1 if step_x else 0))
        def _(i):
            m = nz - i
            far = (m + 1) // 2
            step_z = m % 2 * far + (1 - m % 2) * (nz - far)
            exchange(step_z, step_x).start()

    for n, step in enumerate((-1, 1, 2)):
        ref = w.at[pl.ds(2, 2), :, (x + step + NX) % NX]
        arrived(ref, qxr.at[n])
    query[...] = project(2)
    keys_n = pre_n + rows_n
    for head in range(width // HD):
        cols = pl.ds(head * HD, HD)

        @pl.loop(0, rows_n // TILE)
        def _(i):
            first = pl.multiple_of(i * TILE, TILE)
            scores = lax.dot_general(
                query[pl.ds(first, TILE), cols], cache[0, pl.ds(0, nblk), :, cols].reshape(keys_n, HD),
                (((1,), (1,)), ((), ())), preferred_element_type=F32,
            ) * HD ** (-0.5)
            kpos = lax.broadcasted_iota(jnp.int32, (TILE, keys_n), 1)
            cpos = lax.broadcasted_iota(jnp.int32, (TILE, keys_n), 0) + first
            valid = (kpos < plen) | ((kpos >= pre_n) & (kpos - pre_n <= cpos))
            scores = jnp.where(valid, scores, -jnp.inf)
            top = jnp.max(scores, axis=-1, keepdims=True)
            expo = jnp.exp(scores - top)
            weights = (expo / jnp.sum(expo, axis=-1, keepdims=True)).astype(BF16)
            context[pl.ds(first, TILE), cols] = jnp.dot(
                weights, cache[1, pl.ds(0, nblk), :, cols].reshape(keys_n, HD), preferred_element_type=F32
            ).astype(BF16)

    per = width // (NX * w_refs[3].shape[0])

    def partial(step_y, core):
        owner = (y + step_y) % ny * NC + core
        part = w[3, pl.ds(owner * per, per)].reshape(width, width)
        return lax.dot_general(
            context[...], part, (((1,), (1,)), ((), ())), preferred_element_type=F32
        )

    order = (2, 1, 3, 0)
    for step in order:
        sib_send[step] = partial(step, 1 - c).astype(BF16)
        send(sib_send.at[step], sib_recv.at[step], bs.at[step], br.at[step], sibling)
    for step in order:
        mine[step] = partial(step, c)
    for step in order:
        arrived(sib_recv.at[step], br.at[step])
        total = mine[step] + sib_recv[step].astype(F32)
        if step:
            y_send[step - 1] = total.astype(BF16)
            send(y_send.at[step - 1], y_recv.at[step - 1], ys.at[step - 1], yr.at[step - 1], at_y(step))
        else:
            mine[0] = total
    for n in (1, 0, 2):
        arrived(y_recv.at[n], yr.at[n])
    total = mine[0]
    for n in range(ny - 1):
        total = total + y_recv[n].astype(F32)
    attn_out[...] = total.astype(BF16)

    keep.wait()
    for copy in started:
        copy.wait_send()
    arrived(cache_out.at[pl.ds(0, (groups - 1) * cap)], ex.at[1])
    arrived(packed.at[pl.ds(0, (groups - 1) * cap)], ex.at[0])


def body(tokens, w_query, w_key, w_value, w_out, prefix_cache, prefix_len, owners):
    groups, tensors = lax.axis_size("group"), lax.axis_size("tensor")
    nz, ny = groups // NX, tensors // NC
    nblk = owners.shape[0]
    rows, width = tokens.shape
    depth = w_query.shape[0]
    pre_n = prefix_cache.shape[2]
    cap = max(2, 2 * nblk // groups)
    block = (pre_n + rows) // nblk
    vmem = pl.BlockSpec(memory_space=pltpu.VMEM)
    smem = pl.BlockSpec(memory_space=pltpu.SMEM)
    hbm = pl.BlockSpec(memory_space=pltpu.HBM)
    dma = pltpu.SemaphoreType.DMA
    attn_out, decode_cache = pl.pallas_call(
        functools.partial(kernel, nz, ny, cap),
        out_shape=[
            jax.ShapeDtypeStruct((rows, width), BF16),
            jax.ShapeDtypeStruct((groups * cap, 2, block, width), BF16),
        ],
        in_specs=[hbm] * 6 + [smem, vmem],
        out_specs=[vmem, vmem],
        scratch_shapes=[
            pltpu.VMEM((4, nz, NX, depth, width), BF16),
            pltpu.VMEM((rows, width * tensors), BF16),
            pltpu.VMEM((2, pre_n, width), BF16),
            pltpu.VMEM((2, nblk + 1, block, width), BF16),
            pltpu.VMEM((groups * cap, 2, block, width), BF16),
            pltpu.VMEM((1, groups * cap), jnp.int32),
            pltpu.SMEM((1, groups * cap), jnp.int32),
            pltpu.VMEM((rows, width), BF16),
            pltpu.VMEM((rows, width), BF16),
            pltpu.VMEM((ny, rows, width), F32),
            pltpu.VMEM((ny, rows, width), BF16),
            pltpu.VMEM((ny, rows, width), BF16),
            pltpu.VMEM((ny - 1, rows, width), BF16),
            pltpu.VMEM((ny - 1, rows, width), BF16),
            dma((nz,)), dma((nz,)), dma((nz,)), dma((nz,)),
            dma((2, nz)), dma((2, nz)), dma((nz,)), dma((nz,)),
            dma((3,)), dma((3,)), dma((14,)), dma((14,)), dma((8,)),
            dma((ny,)), dma((ny,)), dma((ny - 1,)), dma((ny - 1,)), dma((2,)),
        ],
        compiler_params=pltpu.CompilerParams(
            collective_id=0, has_side_effects=True, vmem_limit_bytes=48 << 20
        ),
    )(w_key, w_value, w_query, w_out.T, tokens, prefix_cache, prefix_len, owners)
    return attn_out, decode_cache[None]


def solution(mesh):
    in_specs = (
        P("group", "tensor"),
        P("group", "tensor"),
        P("group", "tensor"),
        P("group", "tensor"),
        P("tensor", "group"),
        P("group", None, None, "tensor"),
        P("group"),
        P("group", None),
    )
    out_specs = (P("group", "tensor"), P("group", None, None, None, "tensor"))
    return jax.shard_map(body, mesh=mesh, in_specs=in_specs, out_specs=out_specs, check_vma=False)
```

time: 194 us -> 149 us (0.77)
  waiting for transfers between devices: 85.5 us -> 0 us
  Pallas kernels: 60.6 us -> 139 us
  between operations: 14.8 us -> 1.29 us
  starting transfers between devices: 9.08 us -> 0 us
  matrix products: 6.98 us -> 0 us
  local copies, waits for them, and re-layouts: 13.8 us -> 7.63 us
  other arithmetic: 2.37 us -> 0 us
    all_to_all x1 -> x0, waiting for transfers between devices: 85.5 us -> none  [body(): lax.all_to_all(send, 'group', split_axis=0, concat_axis=0, tiled=True)]
    pallas_call x2 -> x1, Pallas kernels: 60.6 us -> 139 us  [body(): pl.pallas_call(functools.partial(kernel, nz, ny, cap), out_shape=[jax.Sha...]
    all_to_all x1 -> x0, starting transfers between devices: 9.04 us -> none  [body(): lax.all_to_all(send, 'group', split_axis=0, concat_axis=0, tiled=True)]
    dot_general x4 -> x0, matrix products: 6.98 us -> none  [the longest x1 3.34 us: body(): lax.dot_general(context, w_all[3], (((1,), (1,)), ((), ())), preferred_el...]
    unnamed x21 -> x15, local copies, waits for them, and re-layouts: 10.8 us -> 7.63 us
    slice x3 -> x0, local copies, waits for them, and re-layouts: 2.57 us -> none  [the longest x2 2.54 us: attend(): prefix[1]]
    sub x2 -> x0, other arithmetic: 1.98 us -> none  [the longest x1 1.98 us: attend(): expo = jnp.exp(scores - top)]
  transfers between devices with their start and end apart: 2 -> 0, of which waited for: 1 -> 0; matrix products, arithmetic and copies ran while one was open for 6% -> 0% of each run, Pallas kernels for 0% -> 0%
where the time goes in v2:
time: 149 us; the launch traced here: 148 us
  Pallas kernels  139 us (93%)
  local copies, waits for them, and re-layouts  7.63 us (5%)
    pallas_call x1, Pallas kernels, body(): pl.pallas_call(functools.partial(kernel, nz, ny, cap), out_shape=[jax.Sha...  139 us
    unnamed x15, local copies, waits for them, and re-layouts  7.63 us

profile of v2, /device:TPU:24, one launch (start us, length us, event | category | flops | bytes accessed | tf_op | source)
XLA Modules:
  0.0 148.2 jit_solution(15369175532862985454)
XLA Ops:
  1.3 0.7 copy.10.refs_7_
  2.0 0.0 copy-start
  2.0 1.0 copy-done
  3.1 0.0 copy-start.1
  3.1 0.9 copy-done.1
  4.0 0.0 copy-start.2
  4.0 0.7 copy-done.2
  4.7 0.0 copy-start.3
  4.7 0.7 copy-done.3
  5.5 0.0 copy-start.4
  5.5 0.7 copy-done.4
  6.2 0.0 copy-start.5
  6.2 0.7 copy-done.5
  6.9 139.3 %shard_map.95 = (bf16[512,256]{1,0:T(8,128)(2,1)S(1)}, bf16[128,2,16,256]{3,2,1,0:T(8,128)(2,1)S(1)}) custom-call(bf16[32,256]{1,0:T(8,128)(2,1)S(1)} %copy-done.2, bf16[32,256]{1,0:T(8,128)(2,1)S(1)} %copy-done.3, bf16[32,256]{1,0:T(8,128)(2,1)S(1)} %copy-done.4, bf16[32,256]{1,0:T(8,128)(2,1)S(1)} %bitcast.3, bf16[512,256]{1,0:T(8,128)(2,1)S(1)} %copy-done.1, ...), custom_call_target="tpu_custom_call" | custom-call | tf_op jit(solution)/shard_map/pallas_call | solution.py:320
  146.1 0.7 copy.14
  146.9 1.3 copy.15
Async XLA Ops:
  2.0 1.0 copy-start
  3.1 0.9 copy-start.1
  4.0 0.7 copy-start.2
  4.7 0.7 copy-start.3
  5.5 0.7 copy-start.4
  6.2 0.7 copy-start.5

commit v3 on v2

--- a/solution.py
+++ b/solution.py
@@ -21,7 +21,9 @@
     attn_out, cache_out = refs[8:10]
     w, tok, pre, cache, packed, where_v, where_s, query, context = refs[10:19]
     mine, sib_send, sib_recv, y_send, y_recv = refs[19:24]
-    zs, zr, qzs, qzr, xs, xr, ds, dr, qxs, qxr, ts, tr, loc, bs, br, ys, yr, ex = refs[24:]
+    relay = refs[24]
+    zs, zr, qzs, qzr, xs, xr, ds, dr, qxs, qxr, ts, tr, loc, bs, br, ys, yr, ex = refs[25:43]
+    rs, rr, fs = refs[43:]
 
     g, t = lax.axis_index("group"), lax.axis_index("tensor")
     z, x = g // NX, g % NX
@@ -30,7 +32,7 @@
     rows_n, width = tok_ref.shape
     half = rows_n // 2
     pre_n = pre_ref.shape[2]
-    nblk = own_ref.shape[0]
+    nblk = own_ref.shape[1]
     block = (pre_n + rows_n) // nblk
     up, down = nz // 2, (nz - 1) // 2
 
@@ -85,31 +87,31 @@
     def z_of(k):
         return (z - k + nz) % nz if k <= up else (z + (k - up)) % nz
 
-    def kv(k, step_x):
-        return w.at[pl.ds(0, 2), z_of(k), (x + step_x + NX) % NX]
-
-    def qo(k):
-        return w.at[pl.ds(2, 2), z_of(k), x]
+    def key_rows(k, step_x):
+        return w.at[0, z_of(k), (x + step_x + NX) % NX]
+
+    def other_rows(k):
+        return w.at[pl.ds(1, 3), z_of(k), x]
 
     def along_z(item, k, d, sign, most, ssem, rsem):
         for j in range(min(JUMP, most - d), 0, -1):
             kk = (d + j) if sign > 0 else up + d + j
             send(item(k), item(k), ssem.at[kk], rsem.at[kk], at_z(sign * j))
 
-    def kv_here(k):
-        return kv(k, 0)
+    def key_here(k):
+        return key_rows(k, 0)
 
     def along_x(k):
-        send(kv(k, 0), kv(k, 0), xs.at[0, k], xr.at[0, k], at_x(1))
-        send(kv(k, 0), kv(k, 0), xs.at[1, k], xr.at[1, k], at_x(-1))
+        send(key_rows(k, 0), key_rows(k, 0), xs.at[0, k], xr.at[0, k], at_x(1))
+        send(key_rows(k, 0), key_rows(k, 0), xs.at[1, k], xr.at[1, k], at_x(-1))
 
     def across_x(k):
-        arrived(kv(k, -1), xr.at[0, k])
-        arrived(kv(k, 1), xr.at[1, k])
+        arrived(key_rows(k, -1), xr.at[0, k])
+        arrived(key_rows(k, 1), xr.at[1, k])
         if k % 2 == 0:
-            send(kv(k, -1), kv(k, -1), ds.at[k], dr.at[k], at_x(1))
+            send(key_rows(k, -1), key_rows(k, -1), ds.at[k], dr.at[k], at_x(1))
         else:
-            send(kv(k, 1), kv(k, 1), ds.at[k], dr.at[k], at_x(-1))
+            send(key_rows(k, 1), key_rows(k, 1), ds.at[k], dr.at[k], at_x(-1))
 
     def tokens(step_y, h, core):
         owner = (y + step_y + ny) % ny * NC + core
@@ -119,20 +121,20 @@
         send(tokens(step_y, h, c), tokens(step_y, h, c), ts.at[n], tr.at[n], sibling)
 
     for sign, most in ((1, up), (-1, down)):
-        along_z(kv_here, 0, 0, sign, most, zs, zr)
+        along_z(key_here, 0, 0, sign, most, zs, zr)
     along_x(0)
     for h in range(2):
         send(tokens(0, h, c), tokens(0, h, c), ts.at[h], tr.at[h], at_y(1))
         send(tokens(0, 1 - h, c), tokens(0, 1 - h, c), ts.at[3 - h], tr.at[3 - h], at_y(-1))
     for sign, most in ((1, up), (-1, down)):
-        along_z(qo, 0, 0, sign, most, qzs, qzr)
+        along_z(other_rows, 0, 0, sign, most, qzs, qzr)
     for h in range(2):
         to_sibling(0, h, 6 + h)
 
-    owner_col = own_ref[...]
+    owner_row = own_ref[...]
     bi = lax.broadcasted_iota(jnp.int32, (nblk, nblk), 0)
     bj = lax.broadcasted_iota(jnp.int32, (nblk, nblk), 1)
-    owner_row = jnp.sum(jnp.where(bi == bj, owner_col, 0), axis=0, keepdims=True)
+    owner_col = jnp.sum(jnp.where(bi == bj, owner_row, 0), axis=1, keepdims=True)
     rank = jnp.sum(
         jnp.where((owner_col == owner_row) & (bj < bi), 1, 0), axis=1, keepdims=True
     )
@@ -180,26 +182,33 @@
             if d > most:
                 continue
             k = d if sign > 0 else up + d
-            arrived(kv(k, 0), zr.at[k])
+            arrived(key_rows(k, 0), zr.at[k])
             if d % JUMP == 0 and d < most:
-                along_z(kv_here, k, d, sign, most, zs, zr)
+                along_z(key_here, k, d, sign, most, zs, zr)
             along_x(k)
             ahead.append((k, d, sign, most))
         for k, dd, sign, most in behind:
             across_x(k)
             if k:
-                arrived(qo(k), qzr.at[k])
+                arrived(other_rows(k), qzr.at[k])
                 if dd % JUMP == 0 and dd < most:
-                    along_z(qo, k, dd, sign, most, qzs, qzr)
+                    along_z(other_rows, k, dd, sign, most, qzs, qzr)
         behind = ahead
         if d in token_at:
             token_step(token_at.index(d))
 
-    for n, step in enumerate((1, -1, 2)):
-        ref = w.at[pl.ds(2, 2), :, x]
-        send(ref, ref, qxs.at[n], qxr.at[n], at_x(step))
+    def cross(first, count, n):
+        ref = w.at[pl.ds(first, count), :, x]
+        for i, step in enumerate((1, -1, 2)):
+            send(ref, ref, qxs.at[n, i], qxr.at[n, i], at_x(step))
+
+    def crossed(first, count, n):
+        for i, step in enumerate((-1, 1, 2)):
+            arrived(w.at[pl.ds(first, count), :, (x + step + NX) % NX], qxr.at[n, i])
+
+    cross(1, 1, 0)
     for k in range(nz):
-        arrived(kv(k, 2), dr.at[k])
+        arrived(key_rows(k, 2), dr.at[k])
     for n, step_y in enumerate((0, 0, -1, -1, 1, 1, 2, 2)):
         arrived(tokens(step_y, n % 2, 1 - c), tr.at[6 + n])
 
@@ -208,42 +217,64 @@
             tok[...], w[i].reshape(tok.shape[1], width), preferred_element_type=F32
         ).astype(BF16)
 
-    for kind in range(2):
+    def pack(kind, peer):
+        for r in range(cap):
+            slot_n = peer * cap + r
+            packed[kind, slot_n] = cache[kind, where_s[0, slot_n]]
+
+    def slots_of(kind, peer):
+        return packed.at[kind, pl.ds(peer * cap, cap)]
+
+    def lands(kind, source):
+        return cache_out.at[pl.ds(source * cap, cap), kind]
+
+    def exchange(kind):
+        for dx in range(NX):
+            peer = (z + up) % nz * NX + (x + dx) % NX
+            pack(kind, peer)
+            n = (kind * 2 + dx % 2) * 2 + dx // 2
+            send(slots_of(kind, peer), relay.at[n], rs.at[n], rr.at[n], at_z(1 - 2 * (dx % 2)))
+        for step_x in (0, 1, 3, 2):
+
+            @pl.loop(1, nz - (0 if step_x else 1))
+            def _(i):
+                m = nz - 1 - i
+                far = (m + 1) // 2
+                step_z = m % 2 * far + (1 - m % 2) * (nz - far)
+                peer = (z + step_z) % nz * NX + (x + step_x) % NX
+                pack(kind, peer)
+                pltpu.make_async_remote_copy(
+                    src_ref=slots_of(kind, peer), dst_ref=lands(kind, g),
+                    send_sem=ex.at[kind, 0], recv_sem=ex.at[kind, 1],
+                    device_id=(peer, t), device_id_type=MESH,
+                ).start()
+
+            if step_x == 1:
+                for dx in range(NX):
+                    n = (kind * 2 + dx % 2) * 2 + dx // 2
+                    back = 1 - 2 * (dx % 2)
+                    arrived(relay.at[n], rr.at[n])
+                    source = (z - back + nz) % nz * NX + x
+                    peer = (z - back + up + nz) % nz * NX + (x + dx) % NX
+                    send(relay.at[n], lands(kind, source), fs.at[n], ex.at[kind, 1], (peer, t))
+        pack(kind, g)
+        keep = pltpu.make_async_copy(slots_of(kind, g), lands(kind, g), loc.at[7 + kind])
+        keep.start()
+        return keep
+
+    def new_rows(kind):
         cache[kind, pl.ds(pre_n // block, rows_n // block)] = project(kind).reshape(
             rows_n // block, block, width
         )
 
-    @pl.loop(0, groups * cap)
-    def _(s):
-        b = where_s[0, s]
-        for kind in range(2):
-            packed[s, kind] = cache[kind, b]
-
-    def exchange(step_z, step_x):
-        peer = (z + step_z) % nz * NX + (x + step_x) % NX
-        return pltpu.make_async_remote_copy(
-            src_ref=packed.at[pl.ds(peer * cap, cap)],
-            dst_ref=cache_out.at[pl.ds(g * cap, cap)],
-            send_sem=ex.at[0], recv_sem=ex.at[1],
-            device_id=(peer, t), device_id_type=MESH,
-        )
-
-    keep = pltpu.make_async_copy(
-        packed.at[pl.ds(g * cap, cap)], cache_out.at[pl.ds(g * cap, cap)], loc.at[7]
-    )
-    keep.start()
-    for step_x in (0, 1, 3, 2):
-
-        @pl.loop(1, nz + (1 if step_x else 0))
-        def _(i):
-            m = nz - i
-            far = (m + 1) // 2
-            step_z = m % 2 * far + (1 - m % 2) * (nz - far)
-            exchange(step_z, step_x).start()
-
-    for n, step in enumerate((-1, 1, 2)):
-        ref = w.at[pl.ds(2, 2), :, (x + step + NX) % NX]
-        arrived(ref, qxr.at[n])
+    new_rows(0)
+    keeps = [exchange(0)]
+    cross(2, 2, 1)
+    crossed(1, 1, 0)
+    new_rows(1)
+    keeps.append(exchange(1))
+
+    crossed(2, 2, 1)
     query[...] = project(2)
     keys_n = pre_n + rows_n
     for head in range(width // HD):
@@ -297,11 +328,13 @@
         total = total + y_recv[n].astype(F32)
     attn_out[...] = total.astype(BF16)
 
-    keep.wait()
+    for keep in keeps:
+        keep.wait()
     for copy in started:
         copy.wait_send()
-    arrived(cache_out.at[pl.ds(0, (groups - 1) * cap)], ex.at[1])
-    arrived(packed.at[pl.ds(0, (groups - 1) * cap)], ex.at[0])
+    for kind in range(2):
+        arrived(packed.at[kind, pl.ds(0, (groups - 1 - NX) * cap)], ex.at[kind, 0])
+        arrived(cache_out.at[pl.ds(0, (groups - 1) * cap), kind], ex.at[kind, 1])
 
 
 def body(tokens, w_query, w_key, w_value, w_out, prefix_cache, prefix_len, owners):
@@ -315,13 +348,13 @@
     block = (pre_n + rows) // nblk
     vmem = pl.BlockSpec(memory_space=pltpu.VMEM)
     smem = pl.BlockSpec(memory_space=pltpu.SMEM)
-    hbm = pl.BlockSpec(memory_space=pltpu.HBM)
+    hbm = pl.BlockSpec(memory_space=pl.ANY)
     dma = pltpu.SemaphoreType.DMA
     attn_out, decode_cache = pl.pallas_call(
         functools.partial(kernel, nz, ny, cap),
         out_shape=[
-            jax.ShapeDtypeStruct((rows, width), BF16),
-            jax.ShapeDtypeStruct((groups * cap, 2, block, width), BF16),
+            pltpu.VMEM((rows, width), BF16),
+            pltpu.VMEM((groups * cap, 2, block, width), BF16),
         ],
         in_specs=[hbm] * 6 + [smem, vmem],
         out_specs=[vmem, vmem],
@@ -330,7 +363,7 @@
             pltpu.VMEM((rows, width * tensors), BF16),
             pltpu.VMEM((2, pre_n, width), BF16),
             pltpu.VMEM((2, nblk + 1, block, width), BF16),
-            pltpu.VMEM((groups * cap, 2, block, width), BF16),
+            pltpu.VMEM((2, groups * cap, block, width), BF16),
             pltpu.VMEM((1, groups * cap), jnp.int32),
             pltpu.SMEM((1, groups * cap), jnp.int32),
             pltpu.VMEM((rows, width), BF16),
@@ -340,15 +373,17 @@
             pltpu.VMEM((ny, rows, width), BF16),
             pltpu.VMEM((ny - 1, rows, width), BF16),
             pltpu.VMEM((ny - 1, rows, width), BF16),
+            pltpu.VMEM((4 * 2, cap, block, width), BF16),
             dma((nz,)), dma((nz,)), dma((nz,)), dma((nz,)),
             dma((2, nz)), dma((2, nz)), dma((nz,)), dma((nz,)),
-            dma((3,)), dma((3,)), dma((14,)), dma((14,)), dma((8,)),
-            dma((ny,)), dma((ny,)), dma((ny - 1,)), dma((ny - 1,)), dma((2,)),
+            dma((2, 3)), dma((2, 3)), dma((14,)), dma((14,)), dma((9,)),
+            dma((ny,)), dma((ny,)), dma((ny - 1,)), dma((ny - 1,)), dma((2, 2)),
+            dma((8,)), dma((8,)), dma((8,)),
         ],
         compiler_params=pltpu.CompilerParams(
-            collective_id=0, has_side_effects=True, vmem_limit_bytes=48 << 20
+            collective_id=0, has_side_effects=True, vmem_limit_bytes=56 << 20
         ),
-    )(w_key, w_value, w_query, w_out.T, tokens, prefix_cache, prefix_len, owners)
+    )(w_key, w_value, w_query, w_out.T, tokens, prefix_cache, prefix_len, owners.reshape(1, nblk))
     return attn_out, decode_cache[None]
 
 

time: 149 us -> 141 us (0.946)
  local copies, waits for them, and re-layouts: 7.63 us -> 2.02 us
  Pallas kernels: 139 us -> 137 us
    unnamed x15 -> x2, local copies, waits for them, and re-layouts: 7.63 us -> 2.02 us
    pallas_call x1, Pallas kernels: 139 us -> 137 us  [body(): pl.pallas_call(functools.partial(kernel, nz, ny, cap), out_shape=[pltpu.V...]
where the time goes in v3:
time: 141 us
  Pallas kernels  137 us (97%)
  local copies, waits for them, and re-layouts  2.02 us (1%)
    pallas_call x1, Pallas kernels, body(): pl.pallas_call(functools.partial(kernel, nz, ny, cap), out_shape=[pltpu.V...  137 us

profile of v3, /device:TPU:24, one launch (start us, length us, event | category | flops | bytes accessed | tf_op | source)
XLA Modules:
  0.0 140.6 jit_solution(12069601602877108867)
XLA Ops:
  1.3 137.3 %shard_map.95 = (bf16[512,256]{1,0:T(8,128)(2,1)S(1)}, bf16[128,2,16,256]{3,2,1,0:T(8,128)(2,1)S(1)}) custom-call(bf16[32,256]{1,0:T(8,128)(2,1)} %refs_0_.1, bf16[32,256]{1,0:T(8,128)(2,1)} %refs_1_.1, bf16[32,256]{1,0:T(8,128)(2,1)} %refs_2_.1, bf16[32,256]{1,0:T(8,128)(2,1)} %bitcast.4, bf16[512,256]{1,0:T(8,128)(2,1)} %refs_4_.1, ...), custom_call_target="tpu_custom_call" | custom-call | tf_op jit(solution)/shard_map/pallas_call | solution.py:353
  138.6 0.7 copy.12
  139.3 1.3 copy.13

commit v4 on v3

--- a/solution.py
+++ b/solution.py
@@ -22,8 +22,8 @@
     w, tok, pre, cache, packed, where_v, where_s, query, context = refs[10:19]
     mine, sib_send, sib_recv, y_send, y_recv = refs[19:24]
     relay = refs[24]
-    zs, zr, qzs, qzr, xs, xr, ds, dr, qxs, qxr, ts, tr, loc, bs, br, ys, yr, ex = refs[25:43]
-    rs, rr, fs = refs[43:]
+    zs, zr, qzs, qzr, xs, xr, ds, dr, qxs, qxr, ts, tr, loc, bs, br, ys, yr, es = refs[25:43]
+    er, rs, rr, fs = refs[43:]
 
     g, t = lax.axis_index("group"), lax.axis_index("tensor")
     z, x = g // NX, g % NX
@@ -197,14 +197,23 @@
         if d in token_at:
             token_step(token_at.index(d))
 
+    def column(first, count, n_z, size_z, step):
+        return w.at[pl.ds(first, count), pl.ds(n_z, size_z), (x + step + NX) % NX]
+
     def cross(first, count, n):
-        ref = w.at[pl.ds(first, count), :, x]
-        for i, step in enumerate((1, -1, 2)):
+        ref = column(first, count, 0, nz, 0)
+        for i, step in enumerate((1, -1)):
             send(ref, ref, qxs.at[n, i], qxr.at[n, i], at_x(step))
 
+    def pass_on(first, count, n):
+        for i, step in enumerate((-1, 1)):
+            arrived(column(first, count, 0, nz, step), qxr.at[n, i])
+            ref = column(first, count, i * (nz // 2), nz // 2, step)
+            send(ref, ref, qxs.at[n, 2 + i], qxr.at[n, 2 + i], at_x(-step))
+
     def crossed(first, count, n):
-        for i, step in enumerate((-1, 1, 2)):
-            arrived(w.at[pl.ds(first, count), :, (x + step + NX) % NX], qxr.at[n, i])
+        for i in range(2):
+            arrived(column(first, count, i * (nz // 2), nz // 2, 2), qxr.at[n, 2 + i])
 
     cross(1, 1, 0)
     for k in range(nz):
@@ -228,39 +237,51 @@
     def lands(kind, source):
         return cache_out.at[pl.ds(source * cap, cap), kind]
 
-    def exchange(kind):
+    columns_x = (0, 1, 3, 2)
+
+    def part_size(j):
+        return nz - 1 - (0 if columns_x[j] else 1)
+
+    def exchange(kind, j):
+        if j == 0:
+            for dx in range(NX):
+                peer = (z + up) % nz * NX + (x + dx) % NX
+                pack(kind, peer)
+                n = (kind * 2 + dx % 2) * 2 + dx // 2
+                send(slots_of(kind, peer), relay.at[n], rs.at[n], rr.at[n], at_z(1 - 2 * (dx % 2)))
+
+        @pl.loop(1, part_size(j) + 1)
+        def _(i):
+            m = nz - 1 - i
+            far = (m + 1) // 2
+            step_z = m % 2 * far + (1 - m % 2) * (nz - far)
+            peer = (z + step_z) % nz * NX + (x + columns_x[j]) % NX
+            pack(kind, peer)
+            pltpu.make_async_remote_copy(
+                src_ref=slots_of(kind, peer), dst_ref=lands(kind, g),
+                send_sem=es.at[kind, j], recv_sem=er.at[kind],
+                device_id=(peer, t), device_id_type=MESH,
+            ).start()
+
+    def sent(kind, j):
+        arrived(packed.at[kind, pl.ds(0, part_size(j) * cap)], es.at[kind, j])
+
+    def relays(kind):
         for dx in range(NX):
-            peer = (z + up) % nz * NX + (x + dx) % NX
-            pack(kind, peer)
             n = (kind * 2 + dx % 2) * 2 + dx // 2
-            send(slots_of(kind, peer), relay.at[n], rs.at[n], rr.at[n], at_z(1 - 2 * (dx % 2)))
-        for step_x in (0, 1, 3, 2):
-
-            @pl.loop(1, nz - (0 if step_x else 1))
-            def _(i):
-                m = nz - 1 - i
-                far = (m + 1) // 2
-                step_z = m % 2 * far + (1 - m % 2) * (nz - far)
-                peer = (z + step_z) % nz * NX + (x + step_x) % NX
-                pack(kind, peer)
-                pltpu.make_async_remote_copy(
-                    src_ref=slots_of(kind, peer), dst_ref=lands(kind, g),
-                    send_sem=ex.at[kind, 0], recv_sem=ex.at[kind, 1],
-                    device_id=(peer, t), device_id_type=MESH,
-                ).start()
-
-            if step_x == 1:
-                for dx in range(NX):
-                    n = (kind * 2 + dx % 2) * 2 + dx // 2
-                    back = 1 - 2 * (dx % 2)
-                    arrived(relay.at[n], rr.at[n])
-                    source = (z - back + nz) % nz * NX + x
-                    peer = (z - back + up + nz) % nz * NX + (x + dx) % NX
-                    send(relay.at[n], lands(kind, source), fs.at[n], ex.at[kind, 1], (peer, t))
+            back = 1 - 2 * (dx % 2)
+            arrived(relay.at[n], rr.at[n])
+            source = (z - back + nz) % nz * NX + x
+            peer = (z - back + up + nz) % nz * NX + (x + dx) % NX
+            send(relay.at[n], lands(kind, source), fs.at[n], er.at[kind], (peer, t))
+
+    keeps = []
+
+    def keep_own(kind):
         pack(kind, g)
-        keep = pltpu.make_async_copy(slots_of(kind, g), lands(kind, g), loc.at[7 + kind])
-        keep.start()
-        return keep
+        copy = pltpu.make_async_copy(slots_of(kind, g), lands(kind, g), loc.at[7 + kind])
+        copy.start()
+        keeps.append(copy)
 
     def new_rows(kind):
         cache[kind, pl.ds(pre_n // block, rows_n // block)] = project(kind).reshape(
@@ -268,11 +289,19 @@
         )
 
     new_rows(0)
-    keeps = [exchange(0)]
+    exchange(0, 0)
     cross(2, 2, 1)
+    exchange(0, 1)
+    keep_own(0)
+    relays(0)
+    pass_on(1, 1, 0)
+    sent(0, 0)
+    exchange(0, 2)
     crossed(1, 1, 0)
     new_rows(1)
-    keeps.append(exchange(1))
+    pass_on(2, 2, 1)
+    sent(0, 1)
+    exchange(0, 3)
 
     crossed(2, 2, 1)
     query[...] = project(2)
@@ -307,12 +336,18 @@
             context[...], part, (((1,), (1,)), ((), ())), preferred_element_type=F32
         )
 
+    sent(0, 2)
+    exchange(1, 0)
+    keep_own(1)
     order = (2, 1, 3, 0)
     for step in order:
         sib_send[step] = partial(step, 1 - c).astype(BF16)
         send(sib_send.at[step], sib_recv.at[step], bs.at[step], br.at[step], sibling)
     for step in order:
         mine[step] = partial(step, c)
+    sent(0, 3)
+    exchange(1, 1)
+    relays(1)
     for step in order:
         arrived(sib_recv.at[step], br.at[step])
         total = mine[step] + sib_recv[step].astype(F32)
@@ -321,6 +356,10 @@
             send(y_send.at[step - 1], y_recv.at[step - 1], ys.at[step - 1], yr.at[step - 1], at_y(step))
         else:
             mine[0] = total
+    sent(1, 0)
+    exchange(1, 2)
+    sent(1, 1)
+    exchange(1, 3)
     for n in (1, 0, 2):
         arrived(y_recv.at[n], yr.at[n])
     total = mine[0]
@@ -332,9 +371,10 @@
         keep.wait()
     for copy in started:
         copy.wait_send()
+    for j in (2, 3):
+        sent(1, j)
     for kind in range(2):
-        arrived(packed.at[kind, pl.ds(0, (groups - 1 - NX) * cap)], ex.at[kind, 0])
-        arrived(cache_out.at[pl.ds(0, (groups - 1) * cap), kind], ex.at[kind, 1])
+        arrived(cache_out.at[pl.ds(0, (groups - 1) * cap), kind], er.at[kind])
 
 
 def body(tokens, w_query, w_key, w_value, w_out, prefix_cache, prefix_len, owners):
@@ -376,9 +416,9 @@
             pltpu.VMEM((4 * 2, cap, block, width), BF16),
             dma((nz,)), dma((nz,)), dma((nz,)), dma((nz,)),
             dma((2, nz)), dma((2, nz)), dma((nz,)), dma((nz,)),
-            dma((2, 3)), dma((2, 3)), dma((14,)), dma((14,)), dma((9,)),
-            dma((ny,)), dma((ny,)), dma((ny - 1,)), dma((ny - 1,)), dma((2, 2)),
-            dma((8,)), dma((8,)), dma((8,)),
+            dma((2, 4)), dma((2, 4)), dma((14,)), dma((14,)), dma((9,)),
+            dma((ny,)), dma((ny,)), dma((ny - 1,)), dma((ny - 1,)), dma((2, NX)),
+            dma((2,)), dma((8,)), dma((8,)), dma((8,)),
         ],
         compiler_params=pltpu.CompilerParams(
             collective_id=0, has_side_effects=True, vmem_limit_bytes=56 << 20

time: 141 us -> 142 us (level)
  no operation moved by 1% of the time
where the time goes in v4:
time: 142 us; the launch traced here: 141 us
  Pallas kernels  137 us (96%)
  local copies, waits for them, and re-layouts  2.02 us (1%)
    pallas_call x1, Pallas kernels, body(): pl.pallas_call(functools.partial(kernel, nz, ny, cap), out_shape=[pltpu.V...  137 us

profile of v4, /device:TPU:24, one launch (start us, length us, event | category | flops | bytes accessed | tf_op | source)
XLA Modules:
  0.0 140.6 jit_solution(12329000711145779558)
XLA Ops:
  1.3 137.3 %shard_map.95 = (bf16[512,256]{1,0:T(8,128)(2,1)S(1)}, bf16[128,2,16,256]{3,2,1,0:T(8,128)(2,1)S(1)}) custom-call(bf16[32,256]{1,0:T(8,128)(2,1)} %refs_0_.1, bf16[32,256]{1,0:T(8,128)(2,1)} %refs_1_.1, bf16[32,256]{1,0:T(8,128)(2,1)} %refs_2_.1, bf16[32,256]{1,0:T(8,128)(2,1)} %bitcast.4, bf16[512,256]{1,0:T(8,128)(2,1)} %refs_4_.1, ...), custom_call_target="tpu_custom_call" | custom-call | tf_op jit(solution)/shard_map/pallas_call | solution.py:393
  138.6 0.7 copy.12
  139.3 1.3 copy.13

commit v5 on v4

--- a/solution.py
+++ b/solution.py
@@ -21,9 +21,9 @@
     attn_out, cache_out = refs[8:10]
     w, tok, pre, cache, packed, where_v, where_s, query, context = refs[10:19]
     mine, sib_send, sib_recv, y_send, y_recv = refs[19:24]
-    relay = refs[24]
-    zs, zr, qzs, qzr, xs, xr, ds, dr, qxs, qxr, ts, tr, loc, bs, br, ys, yr, es = refs[25:43]
-    er, rs, rr, fs = refs[43:]
+    relay, aside = refs[24:26]
+    zs, zr, qzs, qzr, xs, xr, ds, dr, qxs, qxr, ts, tr, loc, bs, br, ys, yr, es = refs[26:44]
+    er, rs, rr, fs, ps, pr = refs[44:]
 
     g, t = lax.axis_index("group"), lax.axis_index("tensor")
     z, x = g // NX, g % NX
@@ -61,15 +61,13 @@
 
     barrier = pltpu.get_barrier_semaphore()
 
-    @pl.loop(1, groups)
-    def _(i):
-        pl.semaphore_signal(barrier, inc=1, device_id=((g + i) % groups, t), device_id_type=MESH)
-
-    for peer in [at_y(i) for i in range(1, ny)] + [sibling]:
+    peers = [at_z(i) for i in range(1, nz)] + [at_x(i) for i in range(1, NX)]
+    peers += [at_y(i) for i in range(1, ny)] + [sibling]
+    for peer in peers:
         pl.semaphore_signal(barrier, inc=1, device_id=peer, device_id_type=MESH)
     for copy in own_copies:
         copy.wait()
-    pl.semaphore_wait(barrier, groups - 1 + ny)
+    pl.semaphore_wait(barrier, len(peers))
 
     started = []
 
@@ -215,7 +213,6 @@
         for i in range(2):
             arrived(column(first, count, i * (nz // 2), nz // 2, 2), qxr.at[n, 2 + i])
 
-    cross(1, 1, 0)
     for k in range(nz):
         arrived(key_rows(k, 2), dr.at[k])
     for n, step_y in enumerate((0, 0, -1, -1, 1, 1, 2, 2)):
@@ -226,62 +223,65 @@
             tok[...], w[i].reshape(tok.shape[1], width), preferred_element_type=F32
         ).astype(BF16)
 
-    def pack(kind, peer):
-        for r in range(cap):
-            slot_n = peer * cap + r
-            packed[kind, slot_n] = cache[kind, where_s[0, slot_n]]
-
-    def slots_of(kind, peer):
-        return packed.at[kind, pl.ds(peer * cap, cap)]
+    columns_x = (0, 1, 3, 2)
+
+    def pack(kind, dx):
+        xi = (x + dx) % NX
+
+        @pl.loop(0, nz)
+        def _(zi):
+            for r in range(cap):
+                packed[kind, zi, xi, r] = cache[kind, where_s[0, (zi * NX + xi) * cap + r]]
 
     def lands(kind, source):
         return cache_out.at[pl.ds(source * cap, cap), kind]
 
-    columns_x = (0, 1, 3, 2)
-
-    def part_size(j):
-        return nz - 1 - (0 if columns_x[j] else 1)
+    def part(kind, j, zi):
+        return aside.at[kind, j - 1, zi] if j else packed.at[kind, zi, x]
+
+    def to_columns(kind):
+        for j in (1, 2, 3):
+            pack(kind, columns_x[j])
+            send(
+                packed.at[kind, :, (x + columns_x[j]) % NX], aside.at[kind, j - 1],
+                ps.at[kind, j - 1], pr.at[kind, j - 1], at_x(columns_x[j]),
+            )
+        pack(kind, 0)
+
+    keeps = []
 
     def exchange(kind, j):
-        if j == 0:
-            for dx in range(NX):
-                peer = (z + up) % nz * NX + (x + dx) % NX
-                pack(kind, peer)
-                n = (kind * 2 + dx % 2) * 2 + dx // 2
-                send(slots_of(kind, peer), relay.at[n], rs.at[n], rr.at[n], at_z(1 - 2 * (dx % 2)))
-
-        @pl.loop(1, part_size(j) + 1)
+        source = z * NX + (x - columns_x[j] + NX) % NX
+        if j:
+            arrived(aside.at[kind, j - 1], pr.at[kind, j - 1])
+        n = kind * NX + j
+        send(part(kind, j, (z + up) % nz), relay.at[n], rs.at[n], rr.at[n], at_z(1 - 2 * (j % 2)))
+
+        @pl.loop(2, nz)
         def _(i):
-            m = nz - 1 - i
+            m = nz - i
             far = (m + 1) // 2
-            step_z = m % 2 * far + (1 - m % 2) * (nz - far)
-            peer = (z + step_z) % nz * NX + (x + columns_x[j]) % NX
-            pack(kind, peer)
+            to_z = (z + m % 2 * far + (1 - m % 2) * (nz - far)) % nz
             pltpu.make_async_remote_copy(
-                src_ref=slots_of(kind, peer), dst_ref=lands(kind, g),
+                src_ref=part(kind, j, to_z), dst_ref=lands(kind, source),
                 send_sem=es.at[kind, j], recv_sem=er.at[kind],
-                device_id=(peer, t), device_id_type=MESH,
+                device_id=(to_z * NX + x, t), device_id_type=MESH,
             ).start()
 
-    def sent(kind, j):
-        arrived(packed.at[kind, pl.ds(0, part_size(j) * cap)], es.at[kind, j])
-
-    def relays(kind):
-        for dx in range(NX):
-            n = (kind * 2 + dx % 2) * 2 + dx // 2
-            back = 1 - 2 * (dx % 2)
-            arrived(relay.at[n], rr.at[n])
-            source = (z - back + nz) % nz * NX + x
-            peer = (z - back + up + nz) % nz * NX + (x + dx) % NX
-            send(relay.at[n], lands(kind, source), fs.at[n], er.at[kind], (peer, t))
-
-    keeps = []
-
-    def keep_own(kind):
-        pack(kind, g)
-        copy = pltpu.make_async_copy(slots_of(kind, g), lands(kind, g), loc.at[7 + kind])
+        copy = pltpu.make_async_copy(part(kind, j, z), lands(kind, source), loc.at[7 + n])
         copy.start()
         keeps.append(copy)
+
+    def sent(kind, j):
+        arrived(packed.at[kind, pl.ds(0, nz - 2), 0], es.at[kind, j])
+
+    def relays(kind, j):
+        n = kind * NX + j
+        back = 1 - 2 * (j % 2)
+        arrived(relay.at[n], rr.at[n])
+        source = (z - back + nz) % nz * NX + (x - columns_x[j] + NX) % NX
+        peer = (z - back + up + nz) % nz * NX + x
+        send(relay.at[n], lands(kind, source), fs.at[n], er.at[kind], (peer, t))
 
     def new_rows(kind):
         cache[kind, pl.ds(pre_n // block, rows_n // block)] = project(kind).reshape(
@@ -289,19 +289,24 @@
         )
 
     new_rows(0)
+    to_columns(0)
     exchange(0, 0)
+    cross(1, 1, 0)
     cross(2, 2, 1)
     exchange(0, 1)
-    keep_own(0)
-    relays(0)
-    pass_on(1, 1, 0)
+    relays(0, 0)
     sent(0, 0)
     exchange(0, 2)
-    crossed(1, 1, 0)
-    new_rows(1)
+    relays(0, 1)
+    pass_on(1, 1, 0)
     pass_on(2, 2, 1)
     sent(0, 1)
     exchange(0, 3)
+    relays(0, 2)
+    crossed(1, 1, 0)
+    new_rows(1)
+    to_columns(1)
+    relays(0, 3)
 
     crossed(2, 2, 1)
     query[...] = project(2)
@@ -338,7 +343,6 @@
 
     sent(0, 2)
     exchange(1, 0)
-    keep_own(1)
     order = (2, 1, 3, 0)
     for step in order:
         sib_send[step] = partial(step, 1 - c).astype(BF16)
@@ -347,7 +351,7 @@
         mine[step] = partial(step, c)
     sent(0, 3)
     exchange(1, 1)
-    relays(1)
+    relays(1, 0)
     for step in order:
         arrived(sib_recv.at[step], br.at[step])
         total = mine[step] + sib_recv[step].astype(F32)
@@ -358,8 +362,11 @@
             mine[0] = total
     sent(1, 0)
     exchange(1, 2)
+    relays(1, 1)
     sent(1, 1)
     exchange(1, 3)
+    relays(1, 2)
+    relays(1, 3)
     for n in (1, 0, 2):
         arrived(y_recv.at[n], yr.at[n])
     total = mine[0]
@@ -374,7 +381,7 @@
     for j in (2, 3):
         sent(1, j)
     for kind in range(2):
-        arrived(cache_out.at[pl.ds(0, (groups - 1) * cap), kind], er.at[kind])
+        arrived(cache_out.at[pl.ds(0, (groups - NX) * cap), kind], er.at[kind])
 
 
 def body(tokens, w_query, w_key, w_value, w_out, prefix_cache, prefix_len, owners):
@@ -403,7 +410,7 @@
             pltpu.VMEM((rows, width * tensors), BF16),
             pltpu.VMEM((2, pre_n, width), BF16),
             pltpu.VMEM((2, nblk + 1, block, width), BF16),
-            pltpu.VMEM((2, groups * cap, block, width), BF16),
+            pltpu.VMEM((2, nz, NX, cap, block, width), BF16),
             pltpu.VMEM((1, groups * cap), jnp.int32),
             pltpu.SMEM((1, groups * cap), jnp.int32),
             pltpu.VMEM((rows, width), BF16),
@@ -413,12 +420,14 @@
             pltpu.VMEM((ny, rows, width), BF16),
             pltpu.VMEM((ny - 1, rows, width), BF16),
             pltpu.VMEM((ny - 1, rows, width), BF16),
-            pltpu.VMEM((4 * 2, cap, block, width), BF16),
+            pltpu.VMEM((2 * NX, cap, block, width), BF16),
+            pltpu.VMEM((2, NX - 1, nz, cap, block, width), BF16),
             dma((nz,)), dma((nz,)), dma((nz,)), dma((nz,)),
             dma((2, nz)), dma((2, nz)), dma((nz,)), dma((nz,)),
-            dma((2, 4)), dma((2, 4)), dma((14,)), dma((14,)), dma((9,)),
+            dma((2, 4)), dma((2, 4)), dma((14,)), dma((14,)), dma((7 + 2 * NX,)),
             dma((ny,)), dma((ny,)), dma((ny - 1,)), dma((ny - 1,)), dma((2, NX)),
             dma((2,)), dma((8,)), dma((8,)), dma((8,)),
+            dma((2, NX - 1)), dma((2, NX - 1)),
         ],
         compiler_params=pltpu.CompilerParams(
             collective_id=0, has_side_effects=True, vmem_limit_bytes=56 << 20

time: 142 us -> 141 us (level); the launches traced: 141 us -> 141 us
  no operation moved by 1% of the time
where the time goes in v5:
time: 141 us
  Pallas kernels  138 us (98%)
  local copies, waits for them, and re-layouts  2.02 us (1%)
    pallas_call x1, Pallas kernels, body(): pl.pallas_call(functools.partial(kernel, nz, ny, cap), out_shape=[pltpu.V...  138 us

profile of v5, /device:TPU:24, one launch (start us, length us, event | category | flops | bytes accessed | tf_op | source)
XLA Modules:
  0.0 141.2 jit_solution(11734244225892669896)
XLA Ops:
  1.3 137.9 %shard_map.95 = (bf16[512,256]{1,0:T(8,128)(2,1)S(1)}, bf16[128,2,16,256]{3,2,1,0:T(8,128)(2,1)S(1)}) custom-call(bf16[32,256]{1,0:T(8,128)(2,1)} %refs_0_.1, bf16[32,256]{1,0:T(8,128)(2,1)} %refs_1_.1, bf16[32,256]{1,0:T(8,128)(2,1)} %refs_2_.1, bf16[32,256]{1,0:T(8,128)(2,1)} %bitcast.4, bf16[512,256]{1,0:T(8,128)(2,1)} %refs_4_.1, ...), custom_call_target="tpu_custom_call" | custom-call | tf_op jit(solution)/shard_map/pallas_call | solution.py:400
  139.2 0.7 copy.12
  139.9 1.3 copy.13

commit v6 on v5

--- a/solution.py
+++ b/solution.py
@@ -91,8 +91,8 @@
     def other_rows(k):
         return w.at[pl.ds(1, 3), z_of(k), x]
 
-    def along_z(item, k, d, sign, most, ssem, rsem):
-        for j in range(min(JUMP, most - d), 0, -1):
+    def along_z(item, k, d, sign, most, ssem, rsem, jump):
+        for j in range(min(jump, most - d), 0, -1):
             kk = (d + j) if sign > 0 else up + d + j
             send(item(k), item(k), ssem.at[kk], rsem.at[kk], at_z(sign * j))
 
@@ -119,13 +119,13 @@
         send(tokens(step_y, h, c), tokens(step_y, h, c), ts.at[n], tr.at[n], sibling)
 
     for sign, most in ((1, up), (-1, down)):
-        along_z(key_here, 0, 0, sign, most, zs, zr)
+        along_z(key_here, 0, 0, sign, most, zs, zr, JUMP)
     along_x(0)
     for h in range(2):
         send(tokens(0, h, c), tokens(0, h, c), ts.at[h], tr.at[h], at_y(1))
         send(tokens(0, 1 - h, c), tokens(0, 1 - h, c), ts.at[3 - h], tr.at[3 - h], at_y(-1))
     for sign, most in ((1, up), (-1, down)):
-        along_z(other_rows, 0, 0, sign, most, qzs, qzr)
+        along_z(other_rows, 0, 0, sign, most, qzs, qzr, 1)
     for h in range(2):
         to_sibling(0, h, 6 + h)
 
@@ -172,7 +172,15 @@
                 arrived(tokens(2, h, c), tr.at[4 + h])
                 to_sibling(2, h, 12 + h)
 
-    behind = [(0, 0, 1, 0)]
+    def others_step(d):
+        for sign, most in ((1, up), (-1, down)):
+            if d <= most:
+                k = d if sign > 0 else up + d
+                arrived(other_rows(k), qzr.at[k])
+                if d < most:
+                    along_z(other_rows, k, d, sign, most, qzs, qzr, 1)
+
+    behind = [0]
     token_at = (up // 2 - 1, up // 2 + 1, up - 1)
     for d in range(1, up + 2):
         ahead = []
@@ -182,18 +190,15 @@
             k = d if sign > 0 else up + d
             arrived(key_rows(k, 0), zr.at[k])
             if d % JUMP == 0 and d < most:
-                along_z(key_here, k, d, sign, most, zs, zr)
+                along_z(key_here, k, d, sign, most, zs, zr, JUMP)
             along_x(k)
-            ahead.append((k, d, sign, most))
-        for k, dd, sign, most in behind:
+            ahead.append(k)
+        for k in behind:
             across_x(k)
-            if k:
-                arrived(other_rows(k), qzr.at[k])
-                if dd % JUMP == 0 and dd < most:
-                    along_z(other_rows, k, dd, sign, most, qzs, qzr)
         behind = ahead
         if d in token_at:
             token_step(token_at.index(d))
+            others_step(1 + token_at.index(d))
 
     def column(first, count, n_z, size_z, step):
         return w.at[pl.ds(first, count), pl.ds(n_z, size_z), (x + step + NX) % NX]
@@ -213,8 +218,10 @@
         for i in range(2):
             arrived(column(first, count, i * (nz // 2), nz // 2, 2), qxr.at[n, 2 + i])
 
+    others_step(up // 2)
     for k in range(nz):
         arrived(key_rows(k, 2), dr.at[k])
+    others_step(up // 2 + 1)
     for n, step_y in enumerate((0, 0, -1, -1, 1, 1, 2, 2)):
         arrived(tokens(step_y, n % 2, 1 - c), tr.at[6 + n])
 
@@ -288,8 +295,11 @@
             rows_n // block, block, width
         )
 
+    others_step(up // 2 + 2)
     new_rows(0)
+    others_step(up // 2 + 3)
     to_columns(0)
+    others_step(up)
     exchange(0, 0)
     cross(1, 1, 0)
     cross(2, 2, 1)

time: 141 us -> 144 us (1.021)
  Pallas kernels: 138 us -> 141 us
    pallas_call x1, Pallas kernels: 138 us -> 141 us  [body(): pl.pallas_call(functools.partial(kernel, nz, ny, cap), out_shape=[pltpu.V...]
where the time goes in v6:
time: 144 us
  Pallas kernels  141 us (98%)
  local copies, waits for them, and re-layouts  2.02 us (1%)
    pallas_call x1, Pallas kernels, body(): pl.pallas_call(functools.partial(kernel, nz, ny, cap), out_shape=[pltpu.V...  141 us

profile of v6, /device:TPU:24, one launch (start us, length us, event | category | flops | bytes accessed | tf_op | source)
XLA Modules:
  0.0 144.3 jit_solution(6588986485882742011)
XLA Ops:
  1.3 141.0 %shard_map.95 = (bf16[512,256]{1,0:T(8,128)(2,1)S(1)}, bf16[128,2,16,256]{3,2,1,0:T(8,128)(2,1)S(1)}) custom-call(bf16[32,256]{1,0:T(8,128)(2,1)} %refs_0_.1, bf16[32,256]{1,0:T(8,128)(2,1)} %refs_1_.1, bf16[32,256]{1,0:T(8,128)(2,1)} %refs_2_.1, bf16[32,256]{1,0:T(8,128)(2,1)} %bitcast.4, bf16[512,256]{1,0:T(8,128)(2,1)} %refs_4_.1, ...), custom_call_target="tpu_custom_call" | custom-call | tf_op jit(solution)/shard_map/pallas_call | solution.py:410
  142.3 0.7 copy.12
  143.0 1.3 copy.13
